TPU v7x, 128 devices: a whole 4x4x4 slice. The times are simulated.
128 devices in a mesh: grp: 8 (over x_lo, z), dp: 16 (over y, x_hi, core).
Axes of the slice: x: 4 (x_hi: 2, x_lo: 2; x = x_hi * 2 + x_lo), y: 4, z: 4, core: 2. Of those that a mesh axis runs over, the one named last changes fastest.
Arguments:
- hidden: bfloat16 [16, 1024, 4096], P('dp', 'grp'), may hold values from -8 to 8
- queries: bfloat16 [16, 1024, 4096], P('dp', 'grp'), may hold values from -12 to 12
- out_grad: bfloat16 [16, 1024, 4096], P('dp', 'grp'), may hold values from -6 to 6
- key_weight: bfloat16 [4096, 512], replicated, may hold values from -0.25 to 0.25
- value_weight: bfloat16 [4096, 512], replicated, may hold values from -0.09375 to 0.09375
- seq_lengths: int32 [16, 8], P('dp'), may hold values from 0 to 1024, as said below
- seq_group: int32 [16, 8], P('dp'), may hold values from 0 to 7, as said below
- loader_offsets: int32 [16, 8], P('dp'), may hold values from 0 to 1024, as said below
Outputs:
- grad_query: bfloat16 [16, 1024, 4096], P('dp', 'grp')
- grad_hidden: bfloat16 [16, 1024, 4096], P('dp', 'grp')
- grad_key_weight: bfloat16 [4096, 512], P(('grp', 'dp'))
- grad_value_weight: bfloat16 [4096, 512], P(('grp', 'dp'))
Inputs may be any that keep to these rules, and one draw needn't show every extreme that they name: `seq_lengths`: slot lengths are multiples of 128; the slots holding a sequence come first and their lengths sum to 1024; other slots have length 0. In every draw some replica holds a single sequence of 1024 rows. `seq_group`: group numbers give the order of the groups; a group may hold several sequences or none. `loader_offsets`: the loader stream of a replica holds its sequences end to end in some order, and an offset is the first row of its sequence there; slots of length 0 have offset 1024.
All inputs are finite; a program needn't handle non-finite values.
Results may differ from a plain program's by a relative error of at most 0.02.
The roundings to bfloat16 on the way count: a program that leaves them out, or rounds other values in their place, can miss the bound.
Values may be sent and summed in bfloat16 or wider, within the bound.
A program may use at most 128 MiB of HBM per device.

v0:
```python
import math

import jax
import jax.numpy as jnp
from jax import lax
from jax.sharding import PartitionSpec as P

HQ = 32
KVH = 4
HD = 128


def layout_tables(lengths, groups, offsets, total_rows):
    slot_count = lengths.shape[0]
    slot_ids = jnp.arange(slot_count, dtype=jnp.int32)
    sort_keys = groups * slot_count + slot_ids
    earlier = (sort_keys[None, :] < sort_keys[:, None]).astype(jnp.int32)
    starts = jnp.sum(earlier * lengths[None, :], axis=1)
    row_ids = jnp.arange(total_rows, dtype=jnp.int32)
    inside = (row_ids[:, None] >= starts[None, :]) & (
        row_ids[:, None] < (starts + lengths)[None, :]
    )
    seq_begin = jnp.sum(jnp.where(inside, starts[None, :], 0), axis=1)
    row_shift = jnp.sum(jnp.where(inside, (offsets - starts)[None, :], 0), axis=1)
    return (seq_begin, row_ids + row_shift)


def block_take(rows_all, block_order, pieces):
    shaped = rows_all.reshape((pieces, rows_all.shape[0] // pieces) + rows_all.shape[1:])
    return jnp.take(shaped, block_order, axis=0).reshape(rows_all.shape)


def attend(query_rows, key_rows, value_rows, grad_rows, seq_begin, heads_dev):
    total_rows = query_rows.shape[0]
    block_rows = min(512, total_rows)
    block_count = total_rows // block_rows
    inv_root = 1.0 / math.sqrt(HD)
    query_blocks = query_rows.reshape(block_count, block_rows, heads_dev, HD)
    grad_blocks = grad_rows.reshape(block_count, block_rows, heads_dev, HD)
    begin_blocks = seq_begin.reshape(block_count, block_rows)
    local_ids = jnp.arange(block_rows, dtype=jnp.int32)

    def tile_scores(query_part, begin_part, query_block, key_block):
        key_part = lax.dynamic_slice_in_dim(key_rows, key_block * block_rows, block_rows, 0)
        value_part = lax.dynamic_slice_in_dim(value_rows, key_block * block_rows, block_rows, 0)
        scores = (
            jnp.einsum("qhd,kd->hqk", query_part, key_part, preferred_element_type=jnp.float32)
            * inv_root
        )
        query_ids = query_block * block_rows + local_ids
        key_ids = key_block * block_rows + local_ids
        visible = (key_ids[None, :] <= query_ids[:, None]) & (
            key_ids[None, :] >= begin_part[:, None]
        )
        return (scores, visible[None], key_part, value_part)

    def per_block(carried, query_block):
        key_grad, value_grad = carried
        query_part = query_blocks[query_block]
        grad_part = grad_blocks[query_block]
        begin_part = begin_blocks[query_block]
        first_block = begin_part[0] // block_rows
        last_block = query_block + 1

        def stat_step(key_block, running):
            row_top, row_total = running
            tiled = tile_scores(query_part, begin_part, query_block, key_block)
            new_top = jnp.maximum(row_top, jnp.max(jnp.where(tiled[1], tiled[0], -1e30), axis=2))
            exp_terms = jnp.where(tiled[1], jnp.exp(tiled[0] - new_top[:, :, None]), 0.0)
            return (new_top, row_total * jnp.exp(row_top - new_top) + jnp.sum(exp_terms, axis=2))

        start_stats = (
            jnp.full((heads_dev, block_rows), -1e30, jnp.float32),
            jnp.zeros((heads_dev, block_rows), jnp.float32),
        )
        row_top, row_total = lax.fori_loop(first_block, last_block, stat_step, start_stats)

        def weights_of(scores, visible):
            return (
                jnp.where(visible, jnp.exp(scores - row_top[:, :, None]), 0.0)
                / row_total[:, :, None]
            )

        def out_step(key_block, attended):
            tiled = tile_scores(query_part, begin_part, query_block, key_block)
            weights_low = weights_of(tiled[0], tiled[1]).astype(jnp.bfloat16)
            return attended + jnp.einsum(
                "hqk,kd->qhd", weights_low, tiled[3], preferred_element_type=jnp.float32
            )

        attended = lax.fori_loop(
            first_block, last_block, out_step, jnp.zeros((block_rows, heads_dev, HD), jnp.float32)
        )
        row_delta = jnp.transpose(jnp.sum(grad_part.astype(jnp.float32) * attended, axis=2))

        def back_step(key_block, running):
            query_grad, key_acc, value_acc = running
            tiled = tile_scores(query_part, begin_part, query_block, key_block)
            weights = weights_of(tiled[0], tiled[1])
            weights_low = weights.astype(jnp.bfloat16)
            prob_grad = jnp.einsum(
                "qhd,kd->hqk", grad_part, tiled[3], preferred_element_type=jnp.float32
            )
            dscore = (weights * (prob_grad - row_delta[:, :, None])).astype(jnp.bfloat16)
            query_grad = query_grad + jnp.einsum(
                "hqk,kd->qhd", dscore, tiled[2], preferred_element_type=jnp.float32
            )
            key_term = (
                jnp.einsum("hqk,qhd->kd", dscore, query_part, preferred_element_type=jnp.float32)
                * inv_root
            )
            value_term = jnp.einsum(
                "hqk,qhd->kd", weights_low, grad_part, preferred_element_type=jnp.float32
            )
            row_at = key_block * block_rows
            key_acc = lax.dynamic_update_slice_in_dim(
                key_acc,
                lax.dynamic_slice_in_dim(key_acc, row_at, block_rows, 0) + key_term,
                row_at,
                0,
            )
            value_acc = lax.dynamic_update_slice_in_dim(
                value_acc,
                lax.dynamic_slice_in_dim(value_acc, row_at, block_rows, 0) + value_term,
                row_at,
                0,
            )
            return (query_grad, key_acc, value_acc)

        start_back = (jnp.zeros((block_rows, heads_dev, HD), jnp.float32), key_grad, value_grad)
        query_grad, key_grad, value_grad = lax.fori_loop(
            first_block, last_block, back_step, start_back
        )
        return ((key_grad, value_grad), query_grad * inv_root)

    zero_rows = jnp.zeros((total_rows, HD), jnp.float32)
    (key_grad, value_grad), query_grads = lax.scan(
        per_block, (zero_rows, zero_rows), jnp.arange(block_count, dtype=jnp.int32)
    )
    return (query_grads.reshape(total_rows, heads_dev * HD), key_grad, value_grad)


def on_device(
    hidden, queries, out_grad, key_weight, value_weight, seq_lengths, seq_group, loader_offsets
):
    group_size = lax.axis_size("grp")
    replica_count = lax.axis_size("dp")
    member = lax.axis_index("grp")
    shard_rows = hidden.shape[1]
    total_rows = shard_rows * group_size
    heads_dev = HQ // group_size
    copies = group_size // KVH
    seq_begin, source = layout_tables(seq_lengths[0], seq_group[0], loader_offsets[0], total_rows)
    block_from = source[::shard_rows] // shard_rows
    block_ids = jnp.arange(group_size, dtype=jnp.int32)
    block_back = jnp.sum(
        jnp.where(block_from[None, :] == block_ids[:, None], block_ids[None, :], 0), axis=1
    )
    tokens = hidden[0]
    key_rows = jnp.dot(tokens, key_weight, preferred_element_type=jnp.float32).astype(jnp.bfloat16)
    value_rows = jnp.dot(tokens, value_weight, preferred_element_type=jnp.float32).astype(
        jnp.bfloat16
    )
    query_split = queries[0].reshape(shard_rows, group_size, heads_dev * HD)
    grad_split = out_grad[0].reshape(shard_rows, group_size, heads_dev * HD)
    query_all, grad_all = (
        lax.all_to_all(query_split, "grp", split_axis=1, concat_axis=0, tiled=True),
        lax.all_to_all(grad_split, "grp", split_axis=1, concat_axis=0, tiled=True),
    )
    query_group = block_take(query_all.reshape(total_rows, heads_dev * HD), block_from, group_size)
    grad_group = block_take(grad_all.reshape(total_rows, heads_dev * HD), block_from, group_size)
    key_all, value_all = (
        lax.all_gather(key_rows, "grp", axis=0, tiled=True),
        lax.all_gather(value_rows, "grp", axis=0, tiled=True),
    )
    kv_column = member // copies * HD
    key_mine = lax.dynamic_slice_in_dim(key_all, kv_column, HD, 1)
    value_mine = lax.dynamic_slice_in_dim(value_all, kv_column, HD, 1)
    key_group = block_take(key_mine, block_from, group_size)
    value_group = block_take(value_mine, block_from, group_size)
    query_grad, key_grad, value_grad = attend(
        query_group, key_group, value_group, grad_group, seq_begin, heads_dev
    )
    query_back = lax.all_to_all(
        query_grad.astype(jnp.bfloat16).reshape(total_rows, 1, heads_dev * HD),
        "grp",
        split_axis=0,
        concat_axis=1,
        tiled=True,
    )
    key_loader = block_take(key_grad, block_back, group_size)
    value_loader = block_take(value_grad, block_back, group_size)
    key_back, value_back, key_home, value_home = (
        lax.all_to_all(
            key_grad.reshape(total_rows, 1, HD), "grp", split_axis=0, concat_axis=1, tiled=True
        ),
        lax.all_to_all(
            value_grad.reshape(total_rows, 1, HD), "grp", split_axis=0, concat_axis=1, tiled=True
        ),
        lax.all_to_all(
            key_loader.reshape(total_rows, 1, HD), "grp", split_axis=0, concat_axis=1, tiled=True
        ),
        lax.all_to_all(
            value_loader.reshape(total_rows, 1, HD), "grp", split_axis=0, concat_axis=1, tiled=True
        ),
    )

    def merge_copies(received):
        return (
            jnp.sum(received.reshape(shard_rows, KVH, copies, HD), axis=2)
            .reshape(shard_rows, KVH * HD)
            .astype(jnp.bfloat16)
        )

    key_low = merge_copies(key_back)
    value_low = merge_copies(value_back)
    grad_hidden = (
        jnp.dot(key_low, key_weight.T, preferred_element_type=jnp.float32)
        + jnp.dot(value_low, value_weight.T, preferred_element_type=jnp.float32)
    ).astype(jnp.bfloat16)
    key_merged = merge_copies(key_home)
    value_merged = merge_copies(value_home)
    norm_factor = 1.0 / math.sqrt(total_rows * replica_count)
    key_product = jnp.dot(tokens.T, key_merged, preferred_element_type=jnp.float32)
    value_product = jnp.dot(tokens.T, value_merged, preferred_element_type=jnp.float32)
    key_sum, value_sum = (
        lax.psum_scatter(key_product, ("grp", "dp"), scatter_dimension=0, tiled=True),
        lax.psum_scatter(value_product, ("grp", "dp"), scatter_dimension=0, tiled=True),
    )
    grad_query = query_back.reshape(1, shard_rows, group_size * heads_dev * HD)
    return (
        grad_query,
        grad_hidden[None],
        (key_sum * norm_factor).astype(jnp.bfloat16),
        (value_sum * norm_factor).astype(jnp.bfloat16),
    )


def solution(mesh):
    placed = (
        P("dp", "grp", None),
        P("dp", "grp", None),
        P("dp", "grp", None),
        P(),
        P(),
        P("dp", None),
        P("dp", None),
        P("dp", None),
    )
    return jax.shard_map(
        on_device,
        mesh=mesh,
        in_specs=placed,
        out_specs=(
            P("dp", "grp", None),
            P("dp", "grp", None),
            P(("grp", "dp"), None),
            P(("grp", "dp"), None),
        ),
        check_vma=False,
    )
```

profile of v0, /device:TPU:1, one launch (start us, length us, event | category | flops | bytes accessed | tf_op | source)
XLA Modules:
  0.0 1508.6 jit_solution(13504563570164679792)
XLA Ops:
  8.4 3.6 convolution_convert_fusion.1
  14.0 6.9 all-to-all-start
  20.9 3.6 convolution_convert_fusion
  25.0 1.6 copy.90
  28.0 10.4 all-to-all-done
  38.4 4.6 all-to-all-start.1
  45.1 16.7 %all-to-all-done.1 = bf16[128,8,512]{2,0,1:T(8,128)(2,1)} async-done(((bf16[128,8,512]{2,0,1:T(8,128)(2,1)}), bf16[128,8,512]{2,0,1:T(8,128)(2,1)}, u32[]{:S(2)}, u32[]{:S(2)}) %all-to-all-start.1) | async-done | bytes 1048608 | tf_op jit(solution)/shard_map/all_to_all | solution.py:168
  61.8 1.8 gather_fusion.2
  63.7 1.6 broadcast_select_fusion
  65.3 2.1 reshape_reshape.21
  67.4 2.1 reshape_reshape.19
  69.6 31.7 %all-gather.5.cloned.1.call-done = bf16[1024,512]{1,0:T(8,128)(2,1)} async-done(((bf16[128,512]{1,0:T(8,128)(2,1)}), bf16[1024,512]{1,0:T(8,128)(2,1)}) %all-gather.5.cloned.1.call-update) | async-done | bytes 1048592 | tf_op jit(solution)/shard_map/all_gather | solution.py:174
  106.1 55.5 %while.94 = (s32[]{:T(128)}, f32[1024,128]{1,0:T(8,128)}, f32[1024,128]{1,0:T(8,128)}, bf16[2,512,4,128]{1,3,2,0:T(8,128)(2,1)}, s32[2]{0:T(128)S(1)}, /*index=5...) while((s32[]{:T(128)}, f32[1024,128]{1,0:T(8,128)}, ...), condition=%wide.region_13.16_spmd.clone.clone, body=%wide.region_3.15_spmd.clone.clone.sunk | while | flops 2172589056 | bytes 54743628 | solution.py:137
  114.0 2.1 while.95
  117.4 4.2 while.96
  117.7 3.9 fusion.110
  121.6 2.6 copy.129
  125.8 7.1 while.97
  128.2 1.8 fusion.122
  130.0 2.4 fusion.124
  141.7 2.2 while.95
  145.1 4.2 while.96
  145.4 3.9 fusion.110
  149.4 2.6 copy.129
  153.6 7.1 while.97
  156.0 1.8 fusion.122
  157.8 2.4 fusion.124
  161.6 1.7 gather_fusion.5
  163.4 1.7 gather_fusion.4
  165.3 10.0 all_to_all.106
  175.5 4.5 convolution_bitcast_fusion.2
  179.9 9.0 copy.110
  189.3 9.9 all_to_all.107
  199.3 4.5 convolution_bitcast_fusion.3
  203.8 9.0 copy.108
  213.8 10.8 all_to_all.105
  224.6 4.1 all-to-all-start.3
  230.2 5.9 convert_element_type.106
  236.6 8.0 reduce
  244.6 2.7 reshape.428
  247.3 5.0 all-to-all-start.2
  253.7 3.8 fusion.65
  257.6 2.5 fusion.57
  260.0 5.6 all-to-all-done.2
  265.6 4.3 reshape.429
  271.2 1.6 copy.96
  274.1 579.3 %reduce-scatter.9.cloned.1.call-done = f32[32,512]{1,0:T(8,128)} async-done(((f32[4096,512]{1,0:T(8,128)}), f32[32,512]{1,0:T(8,128)}) %reduce-scatter.9.cloned.1.call-update) | async-done | bytes 65552
  855.1 645.3 %reduce-scatter.7.cloned.1.call-done = f32[32,512]{1,0:T(8,128)} async-done(((f32[4096,512]{1,0:T(8,128)}), f32[32,512]{1,0:T(8,128)}) %reduce-scatter.7.cloned.1.call-update) | async-done | bytes 65552
  (138 shorter events, 46.4 us)
Async XLA Ops:
  7.2 1.2 copy-start
  7.2 4.8 copy-start.6
  7.2 62.4 %all-gather.3.cloned.1.call-start = ((), (), s32[]{:S(2)}) async-start(), calls=%async_computation.9 | async-start | bytes 1179648 | tf_op jit(solution)/shard_map/all_gather | solution.py:173
  14.0 10.6 copy-start.11
  14.0 10.6 copy-start.8
  14.0 10.8 copy-start.10
  14.0 24.4 %all-to-all-start = ((bf16[128,8,512]{2,0,1:T(8,128)(2,1)}), bf16[128,8,512]{2,0,1:T(8,128)(2,1)S(1)}, u32[]{:S(2)}, u32[]{:S(2)}) async-start(bf16[128,8,512]{2,0,1:T(8,128)(2,1)} %copy.89), calls=%async_computation | async-start | bytes 2097152 | tf_op jit(solution)/shard_map/all_to_all | solution.py:167
  20.9 80.3 %all-gather.5.cloned.1.call-start = ((), (), s32[]{:S(2)}) async-start(), calls=%async_computation.10 | async-start | bytes 1179648 | tf_op jit(solution)/shard_map/all_gather | solution.py:174
  38.4 23.5 %all-to-all-start.1 = ((bf16[128,8,512]{2,0,1:T(8,128)(2,1)}), bf16[128,8,512]{2,0,1:T(8,128)(2,1)}, u32[]{:S(2)}, u32[]{:S(2)}) async-start(bf16[128,8,512]{2,0,1:T(8,128)(2,1)} %copy.91), calls=%async_computation.1 | async-start | bytes 2097152 | tf_op jit(solution)/shard_map/all_to_all | solution.py:168
  42.9 810.4 %reduce-scatter.9.cloned.1.call-start = ((), (), s32[]{:S(2)}) async-start(), calls=%async_computation.12 | async-start | bytes 8454144
  106.1 59.0 %copy-start.9 = (pred[8]{0:T(512)(128)(4,1)S(1)}, pred[8]{0:T(512)(128)(4,1)}, u32[]{:S(2)}) copy-start(pred[8]{0:T(512)(128)(4,1)} %compare_and_fusion.3) | copy-start | bytes 28
  126.2 1.3 copy-start.1
  128.2 4.2 copy-start.2
  153.9 1.3 copy-start.1
  156.0 4.2 copy-start.2
  189.0 1311.4 %reduce-scatter.7.cloned.1.call-start = ((), (), s32[]{:S(2)}) async-start(), calls=%async_computation.11 | async-start | bytes 8454144
  212.8 1.0 copy-start.3
  212.8 16.0 %copy-start.7 = (bf16[2,512,4,128]{1,3,2,0:T(8,128)(2,1)S(1)}, bf16[2,512,4,128]{1,3,2,0:T(8,128)(2,1)}, u32[]{:S(2)}) copy-start(bf16[2,512,4,128]{1,3,2,0:T(8,128)(2,1)} %get-tuple-element.667) | copy-start | bytes 3145732
  224.6 22.7 %all-to-all-start.3 = ((f32[1024,1,128]{2,1,0:T(1,128)}), f32[1024,1,128]{2,1,0:T(1,128)}, u32[]{:S(2)}, u32[]{:S(2)}) async-start(f32[1024,1,128]{2,1,0:T(1,128)} %bitcast.21), calls=%async_computation.3 | async-start | bytes 1048576 | tf_op jit(solution)/shard_map/all_to_all | solution.py:194
  244.6 7.7 copy-start.5
  247.3 18.4 %all-to-all-start.2 = ((bf16[8,2,32768]{2,1,0:T(2,128)(2,1)}), bf16[8,2,32768]{2,1,0:T(2,128)(2,1)}, u32[]{:S(2)}, u32[]{:S(2)}) async-start(bf16[8,2,32768]{2,1,0:T(2,128)(2,1)} %reshape.428), calls=%async_computation.2 | async-start | bytes 2097152 | tf_op jit(solution)/shard_map/all_to_all | solution.py:184
  253.7 3.9 copy-start.4
Sparse Core Ops, SparseCore 0:
  12.1 47.4 all-gather.2
  61.3 39.9 all-gather.4
  189.1 664.2 reduce-scatter.8
  855.7 644.6 reduce-scatter.6
where the time goes:
time: 1520 us; the launch traced here: 1510 us
  waiting for transfers between devices  1290 us (85%)
  local copies, waits for them, and re-layouts  75.5 us (5%)
  matrix products  45.3 us (3%)
  blocking collectives  30.7 us (2%)
  other arithmetic  21.9 us (1%)
  starting transfers between devices  21.2 us (1%)
    unnamed x6, waiting for transfers between devices  1220 us
    unnamed x32, local copies, waits for them, and re-layouts  35.4 us
    all_gather x1, waiting for transfers between devices, on_device(): lax.all_gather(value_rows, 'grp', axis=0, tiled=True)  31.7 us
  transfers between devices with their start and end apart: 8, of which 6 were waited for; matrix products, arithmetic and copies ran while one was open for 5% of the time, Pallas kernels for 0%

commit v1 on v0

v1 whole, which is shorter than its diff:
```python
import math

import jax
import jax.numpy as jnp
from jax import lax
from jax.experimental import pallas as pl
from jax.experimental.pallas import tpu as pltpu
from jax.sharding import PartitionSpec as P

HQ = 32
KVH = 4
HD = 128
SLOTS = 8
QBLK = 256
LOW = jnp.bfloat16
FULL = jnp.float32
MESH = pl.DeviceIdType.MESH
NT = (((1,), (1,)), ((), ()))


def each(first, last, step):
    def body(i, carry):
        step(i)
        return carry

    lax.fori_loop(first, last, body, 0)


def layer_kernel(
    group_size,
    replica_count,
    lengths,
    groups,
    offsets,
    hidden,
    queries,
    out_grad,
    key_weight,
    value_weight,
    grad_query,
    grad_hidden,
    grad_key,
    grad_value,
    hid_v,
    kw_v,
    vw_v,
    q_r,
    do_r,
    kv_s,
    kv_r,
    kt_v,
    hid_r,
    hid_t,
    s_v,
    pg_v,
    wl_v,
    ds_v,
    acc,
    dq_s,
    dq_g,
    ex_s,
    ex_r,
    dkv_g,
    prod,
    prod_s,
    rs_r,
    gh_v,
    begin_v,
    load_sem,
    own_sem,
    q_send,
    q_recv,
    do_send,
    do_recv,
    kv_send,
    kv_recv,
    hid_send,
    hid_recv,
    dq_send,
    dq_recv,
    dq_own,
    ex_send,
    ex_recv,
    ag_send,
    ag_recv,
    rs_send,
    rs_recv,
    gh_sem,
):
    me = lax.axis_index("grp")
    rep = lax.axis_index("dp")
    rows = hidden.shape[0]
    total = rows * group_size
    heads = HQ // group_size
    wide = heads * HD
    chunk = hidden.shape[1] // group_size
    piece = chunk // replica_count
    half = me // KVH
    partner = lax.rem(me + KVH, group_size)
    inv_root = 1.0 / math.sqrt(HD)
    exp_scale = inv_root / math.log(2.0)
    blocks = total // QBLK
    per_block = QBLK // rows

    def peer(o):
        return lax.rem(me + o, group_size)

    def origin(o):
        return lax.rem(me - o + group_size, group_size)

    def first_col(device):
        return lax.rem(device, KVH) * (2 * wide) + (device // KVH) * wide

    def rows_of(block):
        return pl.ds(pl.multiple_of(block * rows, rows), rows)

    def cols(at, n):
        return pl.ds(pl.multiple_of(at, n), n)

    load_hid = pltpu.make_async_copy(hidden, hid_v, load_sem.at[0])
    load_kw = pltpu.make_async_copy(key_weight, kw_v, load_sem.at[1])
    load_vw = pltpu.make_async_copy(value_weight, vw_v, load_sem.at[2])
    load_hid.start()
    load_kw.start()
    load_vw.start()

    barrier = pltpu.get_barrier_semaphore()
    each(
        1,
        group_size,
        lambda o: pl.semaphore_signal(
            barrier, inc=1, device_id={"grp": peer(o)}, device_id_type=MESH
        ),
    )
    each(
        1,
        replica_count,
        lambda o: pl.semaphore_signal(
            barrier,
            inc=1,
            device_id={"dp": lax.rem(rep + o, replica_count)},
            device_id_type=MESH,
        ),
    )

    def q_copy(h, o, to):
        dest = peer(o)
        at = rows_of(me if to else origin(o))
        return pltpu.make_async_remote_copy(
            src_ref=queries.at[:, cols(first_col(dest) + h * HD, HD)],
            dst_ref=q_r.at[h, at, :],
            send_sem=q_send.at[h, o],
            recv_sem=q_recv.at[h, o],
            device_id={"grp": dest},
            device_id_type=MESH,
        )

    def do_copy(h, o, to):
        dest = peer(o)
        at = rows_of(me if to else origin(o))
        return pltpu.make_async_remote_copy(
            src_ref=out_grad.at[:, cols(first_col(dest) + h * HD, HD)],
            dst_ref=do_r.at[h, at, :],
            send_sem=do_send.at[h, o],
            recv_sem=do_recv.at[h, o],
            device_id={"grp": dest},
            device_id_type=MESH,
        )

    def kv_copy(o, to):
        dest = peer(o)
        at = rows_of(me if to else origin(o))
        return pltpu.make_async_remote_copy(
            src_ref=kv_s.at[lax.rem(dest, KVH)],
            dst_ref=kv_r.at[:, at, :],
            send_sem=kv_send.at[o],
            recv_sem=kv_recv.at[o],
            device_id={"grp": dest},
            device_id_type=MESH,
        )

    def hid_copy(o, to):
        dest = peer(o)
        at = rows_of(me if to else origin(o))
        return pltpu.make_async_remote_copy(
            src_ref=hidden.at[:, cols(dest * chunk, chunk)],
            dst_ref=hid_r.at[at, :],
            send_sem=hid_send.at[o],
            recv_sem=hid_recv.at[o],
            device_id={"grp": dest},
            device_id_type=MESH,
        )

    def dq_copy(h, o, to):
        dest = peer(o)
        at = first_col(me if to else origin(o)) + h * HD
        return pltpu.make_async_remote_copy(
            src_ref=dq_g.at[h, rows_of(dest), :],
            dst_ref=grad_query.at[:, cols(at, HD)],
            send_sem=dq_send.at[h, o],
            recv_sem=dq_recv.at[h, o],
            device_id={"grp": dest},
            device_id_type=MESH,
        )

    def dq_stay(h):
        return pltpu.make_async_copy(
            dq_g.at[h, rows_of(me), :],
            grad_query.at[:, cols(first_col(me) + h * HD, HD)],
            dq_own.at[h],
        )

    def ex_copy(b):
        at = pl.ds(b * QBLK, QBLK)
        return pltpu.make_async_remote_copy(
            src_ref=ex_s.at[at, :],
            dst_ref=ex_r.at[at, :],
            send_sem=ex_send.at[b],
            recv_sem=ex_recv.at[b],
            device_id={"grp": partner},
            device_id_type=MESH,
        )

    def ag_copy(b, o, to):
        dest = peer(o)
        at = pl.ds(b * per_block, per_block)
        return pltpu.make_async_remote_copy(
            src_ref=dkv_g.at[at, :, cols(me * HD, HD)],
            dst_ref=dkv_g.at[at, :, cols((me if to else origin(o)) * HD, HD)],
            send_sem=ag_send.at[b, o],
            recv_sem=ag_recv.at[b, o],
            device_id={"grp": dest},
            device_id_type=MESH,
        )

    def rs_copy(o):
        dest = lax.rem(rep + o, replica_count)
        return pltpu.make_async_remote_copy(
            src_ref=prod_s.at[pl.ds(pl.multiple_of(dest * piece, piece), piece), :],
            dst_ref=rs_r.at[o],
            send_sem=rs_send.at[o],
            recv_sem=rs_recv.at[o],
            device_id={"dp": dest},
            device_id_type=MESH,
        )

    def own_q(h):
        return pltpu.make_async_copy(
            queries.at[:, cols(first_col(me) + h * HD, HD)],
            q_r.at[h, rows_of(me), :],
            own_sem.at[0, h],
        )

    def own_do(h):
        return pltpu.make_async_copy(
            out_grad.at[:, cols(first_col(me) + h * HD, HD)],
            do_r.at[h, rows_of(me), :],
            own_sem.at[1, h],
        )

    own_hid = pltpu.make_async_copy(
        hidden.at[:, cols(me * chunk, chunk)], hid_r.at[rows_of(me), :], load_sem.at[3]
    )

    def send_heads(first, last):
        def one(i):
            h = i // (group_size - 1)
            o = lax.rem(i, group_size - 1) + 1
            q_copy(h, o, True).start()
            do_copy(h, o, True).start()

        each(first * (group_size - 1), last * (group_size - 1), one)

    pl.semaphore_wait(barrier, group_size - 1 + replica_count - 1)

    send_heads(0, 2)
    for h in range(heads):
        own_q(h).start()
        own_do(h).start()
    own_hid.start()

    load_hid.wait()
    load_kw.wait()
    hid_rows = hid_v[...]

    def project(weight, which):
        for g in range(0, KVH, 2):
            both = jnp.dot(
                hid_rows, weight[:, g * HD : (g + 2) * HD], preferred_element_type=FULL
            ).astype(LOW)
            kv_s[g, which] = both[:, :HD]
            kv_s[g + 1, which] = both[:, HD:]

    project(kw_v, 0)
    load_vw.wait()
    project(vw_v, 1)
    each(1, group_size, lambda o: kv_copy(o, True).start())
    send_heads(2, heads)
    each(1, group_size, lambda o: hid_copy(o, True).start())
    kv_r[:, rows_of(me), :] = kv_s[lax.rem(me, KVH)]

    row_ids = lax.broadcasted_iota(jnp.int32, (1, total), 1)
    begin = jnp.zeros((1, total), jnp.int32)
    for s in range(SLOTS):
        at, size = offsets[0, s], lengths[0, s]
        begin = jnp.where((row_ids >= at) & (row_ids < at + size), at, begin)
    begin_v[...] = begin
    starts = []
    for s in range(SLOTS):
        start = jnp.int32(0)
        for t in range(SLOTS):
            if t < s:
                before = groups[0, t] <= groups[0, s]
            else:
                before = groups[0, t] < groups[0, s]
            if t != s:
                start = start + jnp.where(before, lengths[0, t], 0)
        starts.append(start)

    def source_row(row):
        found = jnp.int32(0)
        for s in range(SLOTS):
            inside = (row >= starts[s]) & (row < starts[s] + lengths[0, s])
            found = found + jnp.where(inside, offsets[0, s] + row - starts[s], 0)
        return found // rows

    sources = [source_row(b * rows) for b in range(group_size)]

    acc[...] = jnp.zeros_like(acc)
    each(1, group_size, lambda o: kv_copy(o, False).wait_recv())
    kt_v[...] = kv_r[0].T

    scale_other = jnp.where(half == 1, inv_root, 1.0).astype(FULL)
    scale_mine = jnp.where(half == 0, inv_root, 1.0).astype(FULL)
    key_ids = lax.broadcasted_iota(jnp.int32, (HD, QBLK), 0)
    lane_ids = lax.broadcasted_iota(jnp.int32, (HD, QBLK), 1)

    def fold(tile):
        return tile.reshape(HD // 8, 8, QBLK)

    def attend(h, b):
        r0 = b * QBLK
        keys = r0 + QBLK
        tiles = keys // HD
        q_blk = q_r[h, r0 : r0 + QBLK, :]
        do_blk = do_r[h, r0 : r0 + QBLK, :]
        begin_row = begin_v[:, r0 : r0 + QBLK]
        s_v[0:keys, :] = lax.dot_general(
            kv_r[0, 0:keys, :], q_blk, NT, preferred_element_type=FULL
        )
        pg_v[0:keys, :] = lax.dot_general(
            kv_r[1, 0:keys, :], do_blk, NT, preferred_element_type=FULL
        )
        top = jnp.full((8, QBLK), -1e30, FULL)
        for j in range(tiles):
            at = slice(j * HD, (j + 1) * HD)
            seen = key_ids + j * HD >= begin_row
            if j * HD >= r0:
                seen = seen & (key_ids + (j * HD - r0) <= lane_ids)
            tile = jnp.where(seen, s_v[at, :], -1e30)
            s_v[at, :] = tile
            top = jnp.maximum(top, jnp.max(fold(tile), axis=0))
        top = jnp.max(top, axis=0, keepdims=True)
        mass = jnp.zeros((8, QBLK), FULL)
        for j in range(tiles):
            at = slice(j * HD, (j + 1) * HD)
            tile = jnp.exp2((s_v[at, :] - top) * exp_scale)
            s_v[at, :] = tile
            mass = mass + jnp.sum(fold(tile), axis=0)
        inverse = 1.0 / jnp.sum(mass, axis=0, keepdims=True)
        delta = jnp.zeros((8, QBLK), FULL)
        for j in range(tiles):
            at = slice(j * HD, (j + 1) * HD)
            weights = s_v[at, :] * inverse
            low = weights.astype(LOW)
            s_v[at, :] = weights
            wl_v[at, :] = low
            delta = delta + jnp.sum(fold(low.astype(FULL) * pg_v[at, :]), axis=0)
        delta = jnp.sum(delta, axis=0, keepdims=True)
        for j in range(tiles):
            at = slice(j * HD, (j + 1) * HD)
            ds_v[at, :] = (s_v[at, :] * (pg_v[at, :] - delta)).astype(LOW)
        acc[1, 0:keys, :] += jnp.dot(wl_v[0:keys, :], do_blk, preferred_element_type=FULL)
        acc[0, 0:keys, :] += jnp.dot(ds_v[0:keys, :], q_blk, preferred_element_type=FULL)
        grad_t = jnp.dot(kt_v[:, 0:keys], ds_v[0:keys, :], preferred_element_type=FULL)
        grad_rows = (grad_t * inv_root).T.astype(LOW)
        for j in range(QBLK // rows):
            dq_s[r0 // rows + j] = grad_rows[j * rows : (j + 1) * rows, :]

    def one_head(h):
        own_q(h).wait()
        own_do(h).wait()

        def arrive(o):
            q_copy(h, o, False).wait_recv()
            do_copy(h, o, False).wait_recv()

        each(1, group_size, arrive)
        for b in reversed(range(blocks)):
            attend(h, b)

            @pl.when(h == heads - 1)
            def _():
                at = slice(b * QBLK, (b + 1) * QBLK)
                ex_s[at, :] = (acc[1 - half, at, :] * scale_other).astype(LOW)
                ex_copy(b).start()

        for b in range(group_size):
            dq_g[h, b * rows : (b + 1) * rows, :] = dq_s[sources[b]]
        each(1, group_size, lambda o: dq_copy(h, o, True).start())
        dq_stay(h).start()

    each(0, heads, one_head)

    for b in reversed(range(blocks)):
        at = slice(b * QBLK, (b + 1) * QBLK)
        ex_copy(b).wait_recv()
        merged = (acc[half, at, :] * scale_mine + ex_r[at, :].astype(FULL)).astype(LOW)
        for j in range(per_block):
            dkv_g[b * per_block + j, :, cols(me * HD, HD)] = merged[
                j * rows : (j + 1) * rows, :
            ]
        each(1, group_size, lambda o: ag_copy(b, o, True).start())

    own_hid.wait()
    each(1, group_size, lambda o: hid_copy(o, False).wait_recv())
    hid_t[...] = hid_r[...].T

    for b in reversed(range(blocks)):
        at = slice(b * QBLK, (b + 1) * QBLK)
        each(1, group_size, lambda o: ag_copy(b, o, False).wait_recv())
        grads = dkv_g[b * per_block : (b + 1) * per_block].reshape(QBLK, 2 * KVH * HD)
        term = jnp.dot(hid_t[:, at], grads, preferred_element_type=FULL)
        if b == blocks - 1:
            prod[...] = term
        elif b > 0:
            prod[...] += term
        else:
            term = prod[...] + term
            prod[...] = term
            prod_s[...] = term.astype(LOW)
    each(1, replica_count, lambda o: rs_copy(o).start())

    mine = sources[0]
    for b in range(1, group_size):
        mine = jnp.where(me == b, sources[b], mine)
    kvw = KVH * HD
    dk_rows = dkv_g[mine, :, 0:kvw]
    dv_rows = dkv_g[mine, :, kvw : 2 * kvw]

    def hidden_tile(t):
        at = pl.ds(pl.multiple_of(t * 512, 512), 512)
        tile = lax.dot_general(
            dk_rows, kw_v[at, :], NT, preferred_element_type=FULL
        ) + lax.dot_general(dv_rows, vw_v[at, :], NT, preferred_element_type=FULL)
        gh_v[:, at] = tile.astype(LOW)

    each(0, hidden.shape[1] // 512, hidden_tile)
    gh_out = pltpu.make_async_copy(gh_v, grad_hidden, gh_sem)
    gh_out.start()

    norm = 1.0 / math.sqrt(total * replica_count)
    own = pl.ds(pl.multiple_of(rep * piece, piece), piece)
    each(1, replica_count, lambda o: rs_copy(o).wait_recv())
    summed = prod[own, :]
    for o in range(1, replica_count):
        summed = summed + rs_r[o].astype(FULL)
    summed = (summed * norm).astype(LOW)
    grad_key[...] = summed[:, 0:kvw]
    grad_value[...] = summed[:, kvw : 2 * kvw]

    gh_out.wait()
    each(1, replica_count, lambda o: rs_copy(o).wait_send())

    def close(o):
        kv_copy(o, True).wait_send()
        hid_copy(o, True).wait_send()
        for h in range(heads):
            q_copy(h, o, True).wait_send()
            do_copy(h, o, True).wait_send()
            dq_copy(h, o, True).wait_send()
            dq_copy(h, o, False).wait_recv()
        for b in range(blocks):
            ag_copy(b, o, True).wait_send()

    each(1, group_size, close)
    for h in range(heads):
        dq_stay(h).wait()
    for b in range(blocks):
        ex_copy(b).wait_send()


def on_device(
    hidden, queries, out_grad, key_weight, value_weight, seq_lengths, seq_group, loader_offsets
):
    group_size = lax.axis_size("grp")
    replica_count = lax.axis_size("dp")
    rows, width = hidden.shape[1:]
    total = rows * group_size
    heads = HQ // group_size
    kvw = KVH * HD
    chunk = width // group_size
    piece = chunk // replica_count
    blocks = total // QBLK
    dma = pltpu.SemaphoreType.DMA
    scratch = [
        pltpu.VMEM((rows, width), LOW),
        pltpu.VMEM((width, kvw), LOW),
        pltpu.VMEM((width, kvw), LOW),
        pltpu.VMEM((heads, total, HD), LOW),
        pltpu.VMEM((heads, total, HD), LOW),
        pltpu.VMEM((KVH, 2, rows, HD), LOW),
        pltpu.VMEM((2, total, HD), LOW),
        pltpu.VMEM((HD, total), LOW),
        pltpu.VMEM((total, chunk), LOW),
        pltpu.VMEM((chunk, total), LOW),
        pltpu.VMEM((total, QBLK), FULL),
        pltpu.VMEM((total, QBLK), FULL),
        pltpu.VMEM((total, QBLK), LOW),
        pltpu.VMEM((total, QBLK), LOW),
        pltpu.VMEM((2, total, HD), FULL),
        pltpu.VMEM((group_size, rows, HD), LOW),
        pltpu.VMEM((heads, total, HD), LOW),
        pltpu.VMEM((total, HD), LOW),
        pltpu.VMEM((total, HD), LOW),
        pltpu.VMEM((group_size, rows, 2 * kvw), LOW),
        pltpu.VMEM((chunk, 2 * kvw), FULL),
        pltpu.VMEM((chunk, 2 * kvw), LOW),
        pltpu.VMEM((replica_count, piece, 2 * kvw), LOW),
        pltpu.VMEM((rows, width), LOW),
        pltpu.VMEM((1, total), jnp.int32),
        dma((4,)),
        dma((2, heads)),
        dma((heads, group_size)),
        dma((heads, group_size)),
        dma((heads, group_size)),
        dma((heads, group_size)),
        dma((group_size,)),
        dma((group_size,)),
        dma((group_size,)),
        dma((group_size,)),
        dma((heads, group_size)),
        dma((heads, group_size)),
        dma((heads,)),
        dma((blocks,)),
        dma((blocks,)),
        dma((blocks, group_size)),
        dma((blocks, group_size)),
        dma((replica_count,)),
        dma((replica_count,)),
        dma,
    ]
    smem = pl.BlockSpec(memory_space=pltpu.SMEM)
    vmem = pl.BlockSpec(memory_space=pltpu.VMEM)
    anywhere = pl.BlockSpec(memory_space=pl.ANY)

    def kernel(*refs):
        layer_kernel(group_size, replica_count, *refs)

    grad_query, grad_hidden, grad_key, grad_value = pl.pallas_call(
        kernel,
        out_shape=(
            jax.ShapeDtypeStruct((rows, HQ * HD), LOW),
            jax.ShapeDtypeStruct((rows, width), LOW),
            jax.ShapeDtypeStruct((piece, kvw), LOW),
            jax.ShapeDtypeStruct((piece, kvw), LOW),
        ),
        in_specs=[smem, smem, smem] + [anywhere] * 5,
        out_specs=(anywhere, anywhere, vmem, vmem),
        scratch_shapes=scratch,
        compiler_params=pltpu.CompilerParams(
            collective_id=0, has_side_effects=True, vmem_limit_bytes=56 * 1024 * 1024
        ),
        name="layer",
    )(
        seq_lengths,
        seq_group,
        loader_offsets,
        hidden[0],
        queries[0],
        out_grad[0],
        key_weight,
        value_weight,
    )
    return (grad_query[None], grad_hidden[None], grad_key, grad_value)


def solution(mesh):
    placed = (
        P("dp", "grp", None),
        P("dp", "grp", None),
        P("dp", "grp", None),
        P(),
        P(),
        P("dp", None),
        P("dp", None),
        P("dp", None),
    )
    return jax.shard_map(
        on_device,
        mesh=mesh,
        in_specs=placed,
        out_specs=(
            P("dp", "grp", None),
            P("dp", "grp", None),
            P(("grp", "dp"), None),
            P(("grp", "dp"), None),
        ),
        check_vma=False,
    )
```

time: 1520 us -> 116 us (0.08)
  waiting for transfers between devices: 1290 us -> 0 us
  Pallas kernels: 0 us -> 109 us
  local copies, waits for them, and re-layouts: 75.5 us -> 5.82 us
  matrix products: 45.3 us -> 0 us
  blocking collectives: 30.7 us -> 0 us
  other arithmetic: 21.9 us -> 0 us
  starting transfers between devices: 21.2 us -> 0 us
    unnamed x6 -> x0, waiting for transfers between devices: 1220 us -> none
    pallas_call x0 -> x1, Pallas kernels: none -> 109 us  [on_device(): pl.pallas_call(kernel, out_shape=(jax.ShapeDtypeStruct((rows, HQ * HD), L...]
    dot_general x20 -> x0, matrix products: 45.3 us -> none  [the longest x2 7.85 us: out_step(): jnp.einsum('hqk,kd->qhd', weights_low, tiled[3], preferred_element_type=j...]
    all_to_all x4 -> x0, waiting for transfers between devices: 32.7 us -> none  [the longest x1 16.7 us: on_device(): lax.all_to_all(grad_split, 'grp', split_axis=1, concat_axis=0, tiled=True)]
    all_gather x2 -> x0, waiting for transfers between devices: 31.7 us -> none  [the longest x1 31.7 us: on_device(): lax.all_gather(value_rows, 'grp', axis=0, tiled=True)]
    all_to_all x3 -> x0, blocking collectives: 30.7 us -> none  [the longest x1 10.8 us: on_device(): lax.all_to_all(value_grad.reshape(total_rows, 1, HD), 'grp', split_axis=0...]
    unnamed x32 -> x8, local copies, waits for them, and re-layouts: 35.4 us -> 5.82 us
    all_to_all x4 -> x0, starting transfers between devices: 20.7 us -> none  [the longest x1 6.92 us: on_device(): lax.all_to_all(query_split, 'grp', split_axis=1, concat_axis=0, tiled=True)]
  transfers between devices with their start and end apart: 8 -> 0, of which waited for: 6 -> 0; matrix products, arithmetic and copies ran while one was open for 5% -> 0% of each run, Pallas kernels for 0% -> 0%
where the time goes in v1:
time: 116 us; the launch traced here: 115 us
  Pallas kernels  109 us (94%)
  local copies, waits for them, and re-layouts  5.82 us (5%)
    pallas_call x1, Pallas kernels, on_device(): pl.pallas_call(kernel, out_shape=(jax.ShapeDtypeStruct((rows, HQ * HD), L...  109 us
    unnamed x8, local copies, waits for them, and re-layouts  5.82 us

profile of v1, /device:TPU:1, one launch (start us, length us, event | category | flops | bytes accessed | tf_op | source)
XLA Modules:
  0.0 115.2 jit_solution(8896743964643346423)
XLA Ops:
  0.6 108.7 %layer.1 = (bf16[128,4096]{1,0:T(8,128)(2,1)}, bf16[128,4096]{1,0:T(8,128)(2,1)}, bf16[32,512]{1,0:T(8,128)(2,1)}, bf16[32,512]{1,0:T(8,128)(2,1)}) custom-call(s32[1,8]{1,0:T(1,128)} %refs_0_.1, s32[1,8]{1,0:T(1,128)} %refs_1_.1, s32[1,8]{1,0:T(1,128)} %refs_2_.1, bf16[128,4096]{1,0:T(8,128)(2,1)} %bitcast.5, bf16[128,4096]{1,0:T(8,128)(2,1)} %bitcast.6, ...), custom_call_target="tpu_custom_call" | custom-call | tf_op jit(solution)/shard_map/layer/pallas_call | solution.py:560
  109.3 0.0 copy-start.1
  109.3 0.0 copy-start
  109.3 2.3 %copy.16 = bf16[1,128,4096]{2,1,0:T(8,128)(2,1)} copy(bf16[1,128,4096]{2,1,0:T(8,128)(2,1)} %bitcast.9) | data formatting | bytes 2097152
  111.6 2.3 %copy.17 = bf16[1,128,4096]{2,1,0:T(8,128)(2,1)} copy(bf16[1,128,4096]{2,1,0:T(8,128)(2,1)} %bitcast.8) | data formatting | bytes 2097152
  113.9 0.0 copy-done.1
  113.9 0.6 copy.18
  114.5 0.0 copy-done
  114.5 0.6 copy.19
Async XLA Ops:
  109.3 4.6 %copy-start.1 = (bf16[32,512]{1,0:T(8,128)(2,1)S(1)}, bf16[32,512]{1,0:T(8,128)(2,1)}, u32[]{:S(2)}) copy-start(bf16[32,512]{1,0:T(8,128)(2,1)} %get-tuple-element.18) | copy-start | bytes 98308
  109.3 5.2 %copy-start = (bf16[32,512]{1,0:T(8,128)(2,1)S(1)}, bf16[32,512]{1,0:T(8,128)(2,1)}, u32[]{:S(2)}) copy-start(bf16[32,512]{1,0:T(8,128)(2,1)} %get-tuple-element.19) | copy-start | bytes 98308

commit v2 on v1

--- a/solution.py
+++ b/solution.py
@@ -12,6 +12,7 @@
 HD = 128
 SLOTS = 8
 QBLK = 256
+ZS = 4
 LOW = jnp.bfloat16
 FULL = jnp.float32
 MESH = pl.DeviceIdType.MESH
@@ -49,7 +50,7 @@
     kv_s,
     kv_r,
     kt_v,
-    hid_r,
+    hid_s,
     hid_t,
     s_v,
     pg_v,
@@ -58,9 +59,11 @@
     acc,
     dq_s,
     dq_g,
-    ex_s,
-    ex_r,
-    dkv_g,
+    dl_s,
+    dl_r,
+    dg_s,
+    dg_r,
+    dkv_all,
     prod,
     prod_s,
     rs_r,
@@ -79,34 +82,45 @@
     dq_send,
     dq_recv,
     dq_own,
-    ex_send,
-    ex_recv,
-    ag_send,
-    ag_recv,
+    dl_send,
+    dl_recv,
+    dg_send,
+    dg_recv,
+    ya_send,
+    ya_recv,
+    yc_send,
+    yc_recv,
     rs_send,
     rs_recv,
     gh_sem,
 ):
     me = lax.axis_index("grp")
     rep = lax.axis_index("dp")
+    x_lo, z = me // ZS, lax.rem(me, ZS)
+    y, x_hi, core = rep // 4, lax.rem(rep // 2, 2), lax.rem(rep, 2)
+    ys = replica_count // 4
+    column = 2 * ys
+    summed_over = 2 * group_size
     rows = hidden.shape[0]
+    width = hidden.shape[1]
     total = rows * group_size
     heads = HQ // group_size
     wide = heads * HD
-    chunk = hidden.shape[1] // group_size
-    piece = chunk // replica_count
-    half = me // KVH
-    partner = lax.rem(me + KVH, group_size)
+    kvw = KVH * HD
+    piece = width // (group_size * replica_count)
     inv_root = 1.0 / math.sqrt(HD)
     exp_scale = inv_root / math.log(2.0)
     blocks = total // QBLK
     per_block = QBLK // rows
 
     def peer(o):
-        return lax.rem(me + o, group_size)
+        return lax.rem(x_lo + o // ZS, 2) * ZS + lax.rem(z + o, ZS)
 
     def origin(o):
-        return lax.rem(me - o + group_size, group_size)
+        return lax.rem(x_lo + o // ZS, 2) * ZS + lax.rem(z - o + 2 * ZS, ZS)
+
+    def place(at_y, at_x_hi, at_core):
+        return (at_y * 2 + at_x_hi) * 2 + at_core
 
     def first_col(device):
         return lax.rem(device, KVH) * (2 * wide) + (device // KVH) * wide
@@ -125,21 +139,31 @@
     load_vw.start()
 
     barrier = pltpu.get_barrier_semaphore()
+
+    def column_peer(o):
+        return place(lax.rem(y + o // 2, ys), x_hi, lax.rem(core + o, 2))
+
+    def column_origin(o):
+        return lax.rem(y - o // 2 + ys, ys), lax.rem(core + o, 2)
+
+    def sum_peer(o):
+        return {
+            "grp": peer(lax.rem(o, group_size)),
+            "dp": place(y, lax.rem(x_hi + o // group_size, 2), core),
+        }
+
     each(
         1,
-        group_size,
+        column,
         lambda o: pl.semaphore_signal(
-            barrier, inc=1, device_id={"grp": peer(o)}, device_id_type=MESH
+            barrier, inc=1, device_id={"dp": column_peer(o)}, device_id_type=MESH
         ),
     )
     each(
         1,
-        replica_count,
+        summed_over,
         lambda o: pl.semaphore_signal(
-            barrier,
-            inc=1,
-            device_id={"dp": lax.rem(rep + o, replica_count)},
-            device_id_type=MESH,
+            barrier, inc=1, device_id=sum_peer(o), device_id_type=MESH
         ),
     )
 
@@ -180,14 +204,14 @@
         )
 
     def hid_copy(o, to):
-        dest = peer(o)
-        at = rows_of(me if to else origin(o))
-        return pltpu.make_async_remote_copy(
-            src_ref=hidden.at[:, cols(dest * chunk, chunk)],
-            dst_ref=hid_r.at[at, :],
+        dest_y, dest_core = lax.rem(y + o // 2, ys), lax.rem(core + o, 2)
+        from_y, from_core = (y, core) if to else column_origin(o)
+        return pltpu.make_async_remote_copy(
+            src_ref=hid_s.at[dest_y * 2 + dest_core],
+            dst_ref=hid_t.at[from_y, :, cols(from_core * rows, rows)],
             send_sem=hid_send.at[o],
             recv_sem=hid_recv.at[o],
-            device_id={"grp": dest},
+            device_id={"dp": column_peer(o)},
             device_id_type=MESH,
         )
 
@@ -210,37 +234,58 @@
             dq_own.at[h],
         )
 
-    def ex_copy(b):
-        at = pl.ds(b * QBLK, QBLK)
-        return pltpu.make_async_remote_copy(
-            src_ref=ex_s.at[at, :],
-            dst_ref=ex_r.at[at, :],
-            send_sem=ex_send.at[b],
-            recv_sem=ex_recv.at[b],
-            device_id={"grp": partner},
-            device_id_type=MESH,
-        )
-
-    def ag_copy(b, o, to):
+    def dl_copy(dest, source):
+        return pltpu.make_async_remote_copy(
+            src_ref=dl_s.at[dest],
+            dst_ref=dl_r.at[source],
+            send_sem=dl_send.at[dest],
+            recv_sem=dl_recv.at[source],
+            device_id={"grp": dest},
+            device_id_type=MESH,
+        )
+
+    def dg_copy(o, to):
         dest = peer(o)
-        at = pl.ds(b * per_block, per_block)
-        return pltpu.make_async_remote_copy(
-            src_ref=dkv_g.at[at, :, cols(me * HD, HD)],
-            dst_ref=dkv_g.at[at, :, cols((me if to else origin(o)) * HD, HD)],
-            send_sem=ag_send.at[b, o],
-            recv_sem=ag_recv.at[b, o],
+        return pltpu.make_async_remote_copy(
+            src_ref=dg_s.at[dest],
+            dst_ref=dg_r.at[me if to else origin(o)],
+            send_sem=dg_send.at[o],
+            recv_sem=dg_recv.at[o],
             device_id={"grp": dest},
             device_id_type=MESH,
         )
 
-    def rs_copy(o):
-        dest = lax.rem(rep + o, replica_count)
-        return pltpu.make_async_remote_copy(
-            src_ref=prod_s.at[pl.ds(pl.multiple_of(dest * piece, piece), piece), :],
-            dst_ref=rs_r.at[o],
-            send_sem=rs_send.at[o],
-            recv_sem=rs_recv.at[o],
-            device_id={"dp": dest},
+    def ya_copy(part, k, to):
+        at = (y if to else lax.rem(y - k + ys, ys)) * 2 + core
+        return pltpu.make_async_remote_copy(
+            src_ref=dkv_all.at[y * 2 + core, part],
+            dst_ref=dkv_all.at[at, part],
+            send_sem=ya_send.at[part, k],
+            recv_sem=ya_recv.at[part, k],
+            device_id={"dp": place(lax.rem(y + k, ys), x_hi, core)},
+            device_id_type=MESH,
+        )
+
+    def yc_copy(part, k, to):
+        from_y = lax.rem(y - k + ys, ys)
+        return pltpu.make_async_remote_copy(
+            src_ref=dkv_all.at[from_y * 2 + core, part],
+            dst_ref=dkv_all.at[from_y * 2 + (core if to else 1 - core), part],
+            send_sem=yc_send.at[part, k],
+            recv_sem=yc_recv.at[part, k],
+            device_id={"dp": place(y, x_hi, 1 - core)},
+            device_id_type=MESH,
+        )
+
+    def rs_copy(part, o):
+        dest = sum_peer(o)
+        at = dest["grp"] * 2 + lax.rem(x_hi + o // group_size, 2)
+        return pltpu.make_async_remote_copy(
+            src_ref=prod_s.at[part, pl.ds(pl.multiple_of(at * piece, piece), piece), :],
+            dst_ref=rs_r.at[part, o],
+            send_sem=rs_send.at[part, o],
+            recv_sem=rs_recv.at[part, o],
+            device_id=dest,
             device_id_type=MESH,
         )
 
@@ -257,10 +302,6 @@
             do_r.at[h, rows_of(me), :],
             own_sem.at[1, h],
         )
-
-    own_hid = pltpu.make_async_copy(
-        hidden.at[:, cols(me * chunk, chunk)], hid_r.at[rows_of(me), :], load_sem.at[3]
-    )
 
     def send_heads(first, last):
         def one(i):
@@ -271,13 +312,12 @@
 
         each(first * (group_size - 1), last * (group_size - 1), one)
 
-    pl.semaphore_wait(barrier, group_size - 1 + replica_count - 1)
+    pl.semaphore_wait(barrier, column - 1 + summed_over - 1)
 
     send_heads(0, 2)
     for h in range(heads):
         own_q(h).start()
         own_do(h).start()
-    own_hid.start()
 
     load_hid.wait()
     load_kw.wait()
@@ -296,8 +336,22 @@
     project(vw_v, 1)
     each(1, group_size, lambda o: kv_copy(o, True).start())
     send_heads(2, heads)
-    each(1, group_size, lambda o: hid_copy(o, True).start())
     kv_r[:, rows_of(me), :] = kv_s[lax.rem(me, KVH)]
+
+    lanes = 4 * piece
+
+    def turn(t):
+        turned = hid_v[:, cols(t * lanes, lanes)].T
+        g = t // ys
+        to_y = lax.rem(t, ys)
+        for xh in range(2):
+            at = pl.ds(pl.multiple_of((g * 2 + xh) * piece, piece), piece)
+            for c in range(2):
+                hid_s[to_y * 2 + c, at, :] = turned[(xh * 2 + c) * piece :][:piece]
+
+    each(0, width // lanes, turn)
+    each(1, column, lambda o: hid_copy(o, True).start())
+    hid_t[y, :, cols(core * rows, rows)] = hid_s[y * 2 + core]
 
     row_ids = lax.broadcasted_iota(jnp.int32, (1, total), 1)
     begin = jnp.zeros((1, total), jnp.int32)
@@ -317,21 +371,19 @@
                 start = start + jnp.where(before, lengths[0, t], 0)
         starts.append(start)
 
-    def source_row(row):
+    def source_block(row):
         found = jnp.int32(0)
         for s in range(SLOTS):
             inside = (row >= starts[s]) & (row < starts[s] + lengths[0, s])
             found = found + jnp.where(inside, offsets[0, s] + row - starts[s], 0)
         return found // rows
 
-    sources = [source_row(b * rows) for b in range(group_size)]
+    sources = [source_block(b * rows) for b in range(group_size)]
 
     acc[...] = jnp.zeros_like(acc)
     each(1, group_size, lambda o: kv_copy(o, False).wait_recv())
     kt_v[...] = kv_r[0].T
 
-    scale_other = jnp.where(half == 1, inv_root, 1.0).astype(FULL)
-    scale_mine = jnp.where(half == 0, inv_root, 1.0).astype(FULL)
     key_ids = lax.broadcasted_iota(jnp.int32, (HD, QBLK), 0)
     lane_ids = lax.broadcasted_iota(jnp.int32, (HD, QBLK), 1)
 
@@ -384,8 +436,12 @@
         acc[0, 0:keys, :] += jnp.dot(ds_v[0:keys, :], q_blk, preferred_element_type=FULL)
         grad_t = jnp.dot(kt_v[:, 0:keys], ds_v[0:keys, :], preferred_element_type=FULL)
         grad_rows = (grad_t * inv_root).T.astype(LOW)
-        for j in range(QBLK // rows):
+        for j in range(per_block):
             dq_s[r0 // rows + j] = grad_rows[j * rows : (j + 1) * rows, :]
+
+    def send_dq(h):
+        each(1, group_size, lambda o: dq_copy(h, o, True).start())
+        dq_stay(h).start()
 
     def one_head(h):
         own_q(h).wait()
@@ -396,57 +452,74 @@
             do_copy(h, o, False).wait_recv()
 
         each(1, group_size, arrive)
+
+        @pl.when(h == heads - 1)
+        def _():
+            each(0, heads // 2, send_dq)
+
         for b in reversed(range(blocks)):
             attend(h, b)
 
             @pl.when(h == heads - 1)
             def _():
-                at = slice(b * QBLK, (b + 1) * QBLK)
-                ex_s[at, :] = (acc[1 - half, at, :] * scale_other).astype(LOW)
-                ex_copy(b).start()
+                for j in range(b * per_block, (b + 1) * per_block):
+                    at = slice(j * rows, (j + 1) * rows)
+                    dl_s[j, 0] = (acc[0, at, :] * inv_root).astype(LOW)
+                    dl_s[j, 1] = acc[1, at, :].astype(LOW)
+
+                    @pl.when(me != j)
+                    def _():
+                        dl_copy(j, me).start()
 
         for b in range(group_size):
             dq_g[h, b * rows : (b + 1) * rows, :] = dq_s[sources[b]]
-        each(1, group_size, lambda o: dq_copy(h, o, True).start())
-        dq_stay(h).start()
 
     each(0, heads, one_head)
 
-    for b in reversed(range(blocks)):
-        at = slice(b * QBLK, (b + 1) * QBLK)
-        ex_copy(b).wait_recv()
-        merged = (acc[half, at, :] * scale_mine + ex_r[at, :].astype(FULL)).astype(LOW)
-        for j in range(per_block):
-            dkv_g[b * per_block + j, :, cols(me * HD, HD)] = merged[
-                j * rows : (j + 1) * rows, :
-            ]
-        each(1, group_size, lambda o: ag_copy(b, o, True).start())
-
-    own_hid.wait()
-    each(1, group_size, lambda o: hid_copy(o, False).wait_recv())
-    hid_t[...] = hid_r[...].T
-
-    for b in reversed(range(blocks)):
-        at = slice(b * QBLK, (b + 1) * QBLK)
-        each(1, group_size, lambda o: ag_copy(b, o, False).wait_recv())
-        grads = dkv_g[b * per_block : (b + 1) * per_block].reshape(QBLK, 2 * KVH * HD)
-        term = jnp.dot(hid_t[:, at], grads, preferred_element_type=FULL)
-        if b == blocks - 1:
-            prod[...] = term
-        elif b > 0:
-            prod[...] += term
-        else:
-            term = prod[...] + term
-            prod[...] = term
-            prod_s[...] = term.astype(LOW)
-    each(1, replica_count, lambda o: rs_copy(o).start())
-
-    mine = sources[0]
-    for b in range(1, group_size):
-        mine = jnp.where(me == b, sources[b], mine)
-    kvw = KVH * HD
-    dk_rows = dkv_g[mine, :, 0:kvw]
-    dv_rows = dkv_g[mine, :, kvw : 2 * kvw]
+    for b in range(group_size):
+        dg_s[b] = dl_s[sources[b]]
+    each(1, group_size, lambda o: dg_copy(o, True).start())
+    each(heads // 2, heads, send_dq)
+
+    dl_r[me] = dl_s[me]
+    for s in range(group_size):
+
+        @pl.when(me != s)
+        def _():
+            dl_copy(s, s).wait_recv()
+
+    def merge(received, part, g):
+        return (
+            received[g, part].astype(FULL) + received[KVH + g, part].astype(FULL)
+        ).astype(LOW)
+
+    for part in range(2):
+        for g in range(KVH):
+            dkv_all[y * 2 + core, part, :, g * HD : (g + 1) * HD] = merge(dl_r, part, g)
+        each(1, ys, lambda k: ya_copy(part, k, True).start())
+        yc_copy(part, 0, True).start()
+
+    each(1, column, lambda o: hid_copy(o, False).wait_recv())
+    for part in range(2):
+        for k in range(1, ys):
+            ya_copy(part, k, False).wait_recv()
+            yc_copy(part, k, True).start()
+        for k in range(ys):
+            yc_copy(part, k, False).wait_recv()
+            from_y = lax.rem(y - k + ys, ys)
+            grads = dkv_all[pl.ds(from_y * 2, 2), part].reshape(2 * rows, kvw)
+            term = jnp.dot(hid_t[from_y], grads, preferred_element_type=FULL)
+            if k > 0:
+                term = prod[part] + term
+            prod[part] = term
+            if k == ys - 1:
+                prod_s[part] = term.astype(LOW)
+        each(1, summed_over, lambda o: rs_copy(part, o).start())
+
+    dg_r[me] = dg_s[me]
+    each(1, group_size, lambda o: dg_copy(o, False).wait_recv())
+    dk_rows = jnp.concatenate([merge(dg_r, 0, g) for g in range(KVH)], axis=1)
+    dv_rows = jnp.concatenate([merge(dg_r, 1, g) for g in range(KVH)], axis=1)
 
     def hidden_tile(t):
         at = pl.ds(pl.multiple_of(t * 512, 512), 512)
@@ -455,39 +528,56 @@
         ) + lax.dot_general(dv_rows, vw_v[at, :], NT, preferred_element_type=FULL)
         gh_v[:, at] = tile.astype(LOW)
 
-    each(0, hidden.shape[1] // 512, hidden_tile)
+    each(0, width // 512, hidden_tile)
     gh_out = pltpu.make_async_copy(gh_v, grad_hidden, gh_sem)
     gh_out.start()
 
     norm = 1.0 / math.sqrt(total * replica_count)
-    own = pl.ds(pl.multiple_of(rep * piece, piece), piece)
-    each(1, replica_count, lambda o: rs_copy(o).wait_recv())
-    summed = prod[own, :]
-    for o in range(1, replica_count):
-        summed = summed + rs_r[o].astype(FULL)
-    summed = (summed * norm).astype(LOW)
-    grad_key[...] = summed[:, 0:kvw]
-    grad_value[...] = summed[:, kvw : 2 * kvw]
+    own = pl.ds(pl.multiple_of((me * 2 + x_hi) * piece, piece), piece)
+    for part, result in ((0, grad_key), (1, grad_value)):
+        each(1, summed_over, lambda o: rs_copy(part, o).wait_recv())
+        summed = prod[part, own, :]
+        for o in range(1, summed_over):
+            summed = summed + rs_r[part, o].astype(FULL)
+        result[...] = (summed * norm).astype(LOW)
 
     gh_out.wait()
-    each(1, replica_count, lambda o: rs_copy(o).wait_send())
 
     def close(o):
         kv_copy(o, True).wait_send()
-        hid_copy(o, True).wait_send()
+        dg_copy(o, True).wait_send()
         for h in range(heads):
             q_copy(h, o, True).wait_send()
             do_copy(h, o, True).wait_send()
             dq_copy(h, o, True).wait_send()
             dq_copy(h, o, False).wait_recv()
-        for b in range(blocks):
-            ag_copy(b, o, True).wait_send()
 
     each(1, group_size, close)
+    each(1, column, lambda o: hid_copy(o, True).wait_send())
+    for s in range(group_size):
+
+        @pl.when(me != s)
+        def _():
+            dl_copy(s, me).wait_send()
+
     for h in range(heads):
         dq_stay(h).wait()
-    for b in range(blocks):
-        ex_copy(b).wait_send()
+    for part in range(2):
+        each(1, ys, lambda k: ya_copy(part, k, True).wait_send())
+        each(0, ys, lambda k: yc_copy(part, k, True).wait_send())
+        each(1, summed_over, lambda o: rs_copy(part, o).wait_send())
+
+
+def hand_over(first, second, third, fourth, *refs):
+    sems = refs[4]
+    copies = [
+        pltpu.make_async_copy(source, refs[i], sems.at[i])
+        for i, source in enumerate((first, second, third, fourth))
+    ]
+    for copy in copies:
+        copy.start()
+    for copy in copies:
+        copy.wait()
 
 
 def on_device(
@@ -499,9 +589,11 @@
     total = rows * group_size
     heads = HQ // group_size
     kvw = KVH * HD
-    chunk = width // group_size
-    piece = chunk // replica_count
+    piece = width // (group_size * replica_count)
     blocks = total // QBLK
+    ys = replica_count // 4
+    column = 2 * ys
+    chunk = width // column
     dma = pltpu.SemaphoreType.DMA
     scratch = [
         pltpu.VMEM((rows, width), LOW),
@@ -512,8 +604,8 @@
         pltpu.VMEM((KVH, 2, rows, HD), LOW),
         pltpu.VMEM((2, total, HD), LOW),
         pltpu.VMEM((HD, total), LOW),
-        pltpu.VMEM((total, chunk), LOW),
-        pltpu.VMEM((chunk, total), LOW),
+        pltpu.VMEM((column, chunk, rows), LOW),
+        pltpu.VMEM((ys, chunk, 2 * rows), LOW),
         pltpu.VMEM((total, QBLK), FULL),
         pltpu.VMEM((total, QBLK), FULL),
         pltpu.VMEM((total, QBLK), LOW),
@@ -521,15 +613,17 @@
         pltpu.VMEM((2, total, HD), FULL),
         pltpu.VMEM((group_size, rows, HD), LOW),
         pltpu.VMEM((heads, total, HD), LOW),
-        pltpu.VMEM((total, HD), LOW),
-        pltpu.VMEM((total, HD), LOW),
-        pltpu.VMEM((group_size, rows, 2 * kvw), LOW),
-        pltpu.VMEM((chunk, 2 * kvw), FULL),
-        pltpu.VMEM((chunk, 2 * kvw), LOW),
-        pltpu.VMEM((replica_count, piece, 2 * kvw), LOW),
+        pltpu.VMEM((group_size, 2, rows, HD), LOW),
+        pltpu.VMEM((group_size, 2, rows, HD), LOW),
+        pltpu.VMEM((group_size, 2, rows, HD), LOW),
+        pltpu.VMEM((group_size, 2, rows, HD), LOW),
+        pltpu.VMEM((column, 2, rows, kvw), LOW),
+        pltpu.VMEM((2, chunk, kvw), FULL),
+        pltpu.VMEM((2, chunk, kvw), LOW),
+        pltpu.VMEM((2, 2 * group_size, piece, kvw), LOW),
         pltpu.VMEM((rows, width), LOW),
         pltpu.VMEM((1, total), jnp.int32),
-        dma((4,)),
+        dma((3,)),
         dma((2, heads)),
         dma((heads, group_size)),
         dma((heads, group_size)),
@@ -537,17 +631,21 @@
         dma((heads, group_size)),
         dma((group_size,)),
         dma((group_size,)),
-        dma((group_size,)),
-        dma((group_size,)),
+        dma((column,)),
+        dma((column,)),
         dma((heads, group_size)),
         dma((heads, group_size)),
         dma((heads,)),
-        dma((blocks,)),
-        dma((blocks,)),
-        dma((blocks, group_size)),
-        dma((blocks, group_size)),
-        dma((replica_count,)),
-        dma((replica_count,)),
+        dma((group_size,)),
+        dma((group_size,)),
+        dma((group_size,)),
+        dma((group_size,)),
+        dma((2, ys)),
+        dma((2, ys)),
+        dma((2, ys)),
+        dma((2, ys)),
+        dma((2, 2 * group_size)),
+        dma((2, 2 * group_size)),
         dma,
     ]
     smem = pl.BlockSpec(memory_space=pltpu.SMEM)
@@ -557,14 +655,15 @@
     def kernel(*refs):
         layer_kernel(group_size, replica_count, *refs)
 
-    grad_query, grad_hidden, grad_key, grad_value = pl.pallas_call(
+    out_shape = (
+        jax.ShapeDtypeStruct((rows, HQ * HD), LOW),
+        jax.ShapeDtypeStruct((rows, width), LOW),
+        jax.ShapeDtypeStruct((piece, kvw), LOW),
+        jax.ShapeDtypeStruct((piece, kvw), LOW),
+    )
+    results = pl.pallas_call(
         kernel,
-        out_shape=(
-            jax.ShapeDtypeStruct((rows, HQ * HD), LOW),
-            jax.ShapeDtypeStruct((rows, width), LOW),
-            jax.ShapeDtypeStruct((piece, kvw), LOW),
-            jax.ShapeDtypeStruct((piece, kvw), LOW),
-        ),
+        out_shape=out_shape,
         in_specs=[smem, smem, smem] + [anywhere] * 5,
         out_specs=(anywhere, anywhere, vmem, vmem),
         scratch_shapes=scratch,
@@ -582,6 +681,14 @@
         key_weight,
         value_weight,
     )
+    grad_query, grad_hidden, grad_key, grad_value = pl.pallas_call(
+        hand_over,
+        out_shape=out_shape,
+        in_specs=[anywhere] * 4,
+        out_specs=[anywhere] * 4,
+        scratch_shapes=[dma((4,))],
+        name="hand_over",
+    )(*results)
     return (grad_query[None], grad_hidden[None], grad_key, grad_value)
 
 

time: 116 us -> 154 us (1.33)
  Pallas kernels: 109 us -> 154 us
  local copies, waits for them, and re-layouts: 5.82 us -> 0 us
    pallas_call x1 -> x2, Pallas kernels: 109 us -> 154 us  [the longest x1 87 us: on_device(): pl.pallas_call(kernel, out_shape=out_shape, in_specs=[smem, smem, smem] +...]
    unnamed x8 -> x0, local copies, waits for them, and re-layouts: 5.82 us -> none
where the time goes in v2:
time: 154 us
  Pallas kernels  154 us (100%)
    pallas_call x1, Pallas kernels, on_device(): pl.pallas_call(kernel, out_shape=out_shape, in_specs=[smem, smem, smem] +...  87 us
    pallas_call x1, Pallas kernels, on_device(): pl.pallas_call(hand_over, out_shape=out_shape, in_specs=[anywhere] * 4, o...  66.7 us

profile of v2, /device:TPU:1, one launch (start us, length us, event | category | flops | bytes accessed | tf_op | source)
XLA Modules:
  0.0 154.3 jit_solution(17093642872231590028)
XLA Ops:
  0.6 87.0 %layer.1 = (bf16[128,4096]{1,0:T(8,128)(2,1)}, bf16[128,4096]{1,0:T(8,128)(2,1)}, bf16[32,512]{1,0:T(8,128)(2,1)}, bf16[32,512]{1,0:T(8,128)(2,1)}) custom-call(s32[1,8]{1,0:T(1,128)} %refs_0_.1, s32[1,8]{1,0:T(1,128)} %refs_1_.1, s32[1,8]{1,0:T(1,128)} %refs_2_.1, bf16[128,4096]{1,0:T(8,128)(2,1)} %bitcast.5, bf16[128,4096]{1,0:T(8,128)(2,1)} %bitcast.6, ...), custom_call_target="tpu_custom_call" | custom-call | tf_op jit(solution)/shard_map/layer/pallas_call | solution.py:664
  87.6 66.7 %hand_over.1 = (bf16[128,4096]{1,0:T(8,128)(2,1)}, bf16[128,4096]{1,0:T(8,128)(2,1)}, bf16[32,512]{1,0:T(8,128)(2,1)}, bf16[32,512]{1,0:T(8,128)(2,1)}) custom-call(bf16[128,4096]{1,0:T(8,128)(2,1)} %get-tuple-element.12.first, bf16[128,4096]{1,0:T(8,128)(2,1)} %get-tuple-element.13.second, bf16[32,512]{1,0:T(8,128)(2,1)} %get-tuple-element.14.third, ...), custom_call_target="tpu_custom_call" | custom-call | tf_op jit(solution)/shard_map/hand_over/pallas_call | solution.py:684

commit v3 on v2

--- a/solution.py
+++ b/solution.py
@@ -13,6 +13,8 @@
 SLOTS = 8
 QBLK = 256
 ZS = 4
+PARTS = 4
+PCOLS = 2 * KVH * HD // PARTS
 LOW = jnp.bfloat16
 FULL = jnp.float32
 MESH = pl.DeviceIdType.MESH
@@ -88,6 +90,8 @@
     dg_recv,
     ya_send,
     ya_recv,
+    yf_send,
+    yf_recv,
     yc_send,
     yc_recv,
     rs_send,
@@ -256,18 +260,33 @@
         )
 
     def ya_copy(part, k, to):
-        at = (y if to else lax.rem(y - k + ys, ys)) * 2 + core
+        step = ys - 1 if k else 1
+        at = (y if to else lax.rem(y + ys - step, ys)) * 2 + core
         return pltpu.make_async_remote_copy(
             src_ref=dkv_all.at[y * 2 + core, part],
             dst_ref=dkv_all.at[at, part],
             send_sem=ya_send.at[part, k],
             recv_sem=ya_recv.at[part, k],
-            device_id={"dp": place(lax.rem(y + k, ys), x_hi, core)},
+            device_id={"dp": place(lax.rem(y + step, ys), x_hi, core)},
+            device_id_type=MESH,
+        )
+
+    def yf_copy(part, k, to):
+        step = ys - 1 if k else 1
+        come = lax.rem(y + ys - step, ys) * 2 + core
+        far = lax.rem(y + 2, ys) * 2 + core
+        half = pl.ds(k * (rows // 2), rows // 2)
+        return pltpu.make_async_remote_copy(
+            src_ref=dkv_all.at[come, part, half],
+            dst_ref=dkv_all.at[come if to else far, part, half],
+            send_sem=yf_send.at[part, k],
+            recv_sem=yf_recv.at[part, k],
+            device_id={"dp": place(lax.rem(y + step, ys), x_hi, core)},
             device_id_type=MESH,
         )
 
     def yc_copy(part, k, to):
-        from_y = lax.rem(y - k + ys, ys)
+        from_y = lax.rem(y + k, ys)
         return pltpu.make_async_remote_copy(
             src_ref=dkv_all.at[from_y * 2 + core, part],
             dst_ref=dkv_all.at[from_y * 2 + (core if to else 1 - core), part],
@@ -311,13 +330,6 @@
             do_copy(h, o, True).start()
 
         each(first * (group_size - 1), last * (group_size - 1), one)
-
-    pl.semaphore_wait(barrier, column - 1 + summed_over - 1)
-
-    send_heads(0, 2)
-    for h in range(heads):
-        own_q(h).start()
-        own_do(h).start()
 
     load_hid.wait()
     load_kw.wait()
@@ -334,8 +346,14 @@
     project(kw_v, 0)
     load_vw.wait()
     project(vw_v, 1)
+
+    pl.semaphore_wait(barrier, column - 1 + summed_over - 1)
+
     each(1, group_size, lambda o: kv_copy(o, True).start())
-    send_heads(2, heads)
+    send_heads(0, heads)
+    for h in range(heads):
+        own_q(h).start()
+        own_do(h).start()
     kv_r[:, rows_of(me), :] = kv_s[lax.rem(me, KVH)]
 
     lanes = 4 * piece
@@ -453,10 +471,6 @@
 
         each(1, group_size, arrive)
 
-        @pl.when(h == heads - 1)
-        def _():
-            each(0, heads // 2, send_dq)
-
         for b in reversed(range(blocks)):
             attend(h, b)
 
@@ -479,7 +493,7 @@
     for b in range(group_size):
         dg_s[b] = dl_s[sources[b]]
     each(1, group_size, lambda o: dg_copy(o, True).start())
-    each(heads // 2, heads, send_dq)
+    each(0, heads, send_dq)
 
     dl_r[me] = dl_s[me]
     for s in range(group_size):
@@ -493,28 +507,54 @@
             received[g, part].astype(FULL) + received[KVH + g, part].astype(FULL)
         ).astype(LOW)
 
-    for part in range(2):
-        for g in range(KVH):
-            dkv_all[y * 2 + core, part, :, g * HD : (g + 1) * HD] = merge(dl_r, part, g)
-        each(1, ys, lambda k: ya_copy(part, k, True).start())
+    for part in range(PARTS):
+        for i in range(PCOLS // HD):
+            dkv_all[y * 2 + core, part, :, i * HD : (i + 1) * HD] = merge(
+                dl_r, part * PCOLS // kvw, (part * PCOLS % kvw) // HD + i
+            )
+        for k in range(2):
+            ya_copy(part, k, True).start()
         yc_copy(part, 0, True).start()
 
+    def close_early(o):
+        kv_copy(o, True).wait_send()
+        for h in range(heads):
+            q_copy(h, o, True).wait_send()
+            do_copy(h, o, True).wait_send()
+
+    each(1, group_size, close_early)
+
     each(1, column, lambda o: hid_copy(o, False).wait_recv())
-    for part in range(2):
-        for k in range(1, ys):
+    def pass_on(part):
+        for k in range(2):
             ya_copy(part, k, False).wait_recv()
-            yc_copy(part, k, True).start()
-        for k in range(ys):
+            yf_copy(part, k, True).start()
+            yc_copy(part, 1 if k else ys - 1, True).start()
+
+    def hand_far(part):
+        for k in range(2):
+            yf_copy(part, k, False).wait_recv()
+        yc_copy(part, 2, True).start()
+
+    def multiply(part):
+        for k in (0, 1, ys - 1, 2):
             yc_copy(part, k, False).wait_recv()
-            from_y = lax.rem(y - k + ys, ys)
-            grads = dkv_all[pl.ds(from_y * 2, 2), part].reshape(2 * rows, kvw)
+            from_y = lax.rem(y + k, ys)
+            grads = dkv_all[pl.ds(from_y * 2, 2), part].reshape(2 * rows, PCOLS)
             term = jnp.dot(hid_t[from_y], grads, preferred_element_type=FULL)
             if k > 0:
                 term = prod[part] + term
             prod[part] = term
-            if k == ys - 1:
+            if k == 2:
                 prod_s[part] = term.astype(LOW)
         each(1, summed_over, lambda o: rs_copy(part, o).start())
+
+    pass_on(0)
+    for part in range(PARTS):
+        if part + 1 < PARTS:
+            pass_on(part + 1)
+        hand_far(part)
+        multiply(part)
 
     dg_r[me] = dg_s[me]
     each(1, group_size, lambda o: dg_copy(o, False).wait_recv())
@@ -532,52 +572,67 @@
     gh_out = pltpu.make_async_copy(gh_v, grad_hidden, gh_sem)
     gh_out.start()
 
+    def close(o):
+        dg_copy(o, True).wait_send()
+        for h in range(heads):
+            dq_copy(h, o, True).wait_send()
+            dq_copy(h, o, False).wait_recv()
+
+    each(1, group_size, close)
+    each(1, column, lambda o: hid_copy(o, True).wait_send())
+    for s in range(group_size):
+
+        @pl.when(me != s)
+        def _():
+            dl_copy(s, me).wait_send()
+
+    for h in range(heads):
+        dq_stay(h).wait()
+    for part in range(PARTS):
+        for k in range(2):
+            ya_copy(part, k, True).wait_send()
+            yf_copy(part, k, True).wait_send()
+        for k in range(ys):
+            yc_copy(part, k, True).wait_send()
+
     norm = 1.0 / math.sqrt(total * replica_count)
     own = pl.ds(pl.multiple_of((me * 2 + x_hi) * piece, piece), piece)
-    for part, result in ((0, grad_key), (1, grad_value)):
+    for part in range(PARTS):
         each(1, summed_over, lambda o: rs_copy(part, o).wait_recv())
         summed = prod[part, own, :]
         for o in range(1, summed_over):
             summed = summed + rs_r[part, o].astype(FULL)
-        result[...] = (summed * norm).astype(LOW)
+        result = grad_value if part * PCOLS >= kvw else grad_key
+        at = part * PCOLS % kvw
+        result[:, at : at + PCOLS] = (summed * norm).astype(LOW)
 
     gh_out.wait()
-
-    def close(o):
-        kv_copy(o, True).wait_send()
-        dg_copy(o, True).wait_send()
-        for h in range(heads):
-            q_copy(h, o, True).wait_send()
-            do_copy(h, o, True).wait_send()
-            dq_copy(h, o, True).wait_send()
-            dq_copy(h, o, False).wait_recv()
-
-    each(1, group_size, close)
-    each(1, column, lambda o: hid_copy(o, True).wait_send())
-    for s in range(group_size):
-
-        @pl.when(me != s)
-        def _():
-            dl_copy(s, me).wait_send()
-
-    for h in range(heads):
-        dq_stay(h).wait()
-    for part in range(2):
-        each(1, ys, lambda k: ya_copy(part, k, True).wait_send())
-        each(0, ys, lambda k: yc_copy(part, k, True).wait_send())
+    for part in range(PARTS):
         each(1, summed_over, lambda o: rs_copy(part, o).wait_send())
 
 
-def hand_over(first, second, third, fourth, *refs):
-    sems = refs[4]
-    copies = [
-        pltpu.make_async_copy(source, refs[i], sems.at[i])
-        for i, source in enumerate((first, second, third, fourth))
-    ]
-    for copy in copies:
-        copy.start()
-    for copy in copies:
-        copy.wait()
+def hand_over(*refs):
+    sources, results = refs[0:4], refs[4:8]
+    held, sems = refs[8:12], refs[12]
+    steps = []
+    for i, (source, result, slot) in enumerate(zip(sources, results, held)):
+        parts = 4 if i < 2 else 1
+        size = source.shape[0] // parts
+        for j in range(parts):
+            at = pl.ds(j * size, size)
+            steps.append(
+                (
+                    pltpu.make_async_copy(source.at[at], slot.at[at], sems.at[0, i, j]),
+                    pltpu.make_async_copy(slot.at[at], result.at[at], sems.at[1, i, j]),
+                )
+            )
+    for load, _ in steps:
+        load.start()
+    for load, store in steps:
+        load.wait()
+        store.start()
+    for _, store in steps:
+        store.wait()
 
 
 def on_device(
@@ -617,10 +672,10 @@
         pltpu.VMEM((group_size, 2, rows, HD), LOW),
         pltpu.VMEM((group_size, 2, rows, HD), LOW),
         pltpu.VMEM((group_size, 2, rows, HD), LOW),
-        pltpu.VMEM((column, 2, rows, kvw), LOW),
-        pltpu.VMEM((2, chunk, kvw), FULL),
-        pltpu.VMEM((2, chunk, kvw), LOW),
-        pltpu.VMEM((2, 2 * group_size, piece, kvw), LOW),
+        pltpu.VMEM((column, PARTS, rows, PCOLS), LOW),
+        pltpu.VMEM((PARTS, chunk, PCOLS), FULL),
+        pltpu.VMEM((PARTS, chunk, PCOLS), LOW),
+        pltpu.VMEM((PARTS, 2 * group_size, piece, PCOLS), LOW),
         pltpu.VMEM((rows, width), LOW),
         pltpu.VMEM((1, total), jnp.int32),
         dma((3,)),
@@ -640,12 +695,14 @@
         dma((group_size,)),
         dma((group_size,)),
         dma((group_size,)),
-        dma((2, ys)),
-        dma((2, ys)),
-        dma((2, ys)),
-        dma((2, ys)),
-        dma((2, 2 * group_size)),
-        dma((2, 2 * group_size)),
+        dma((PARTS, 2)),
+        dma((PARTS, 2)),
+        dma((PARTS, 2)),
+        dma((PARTS, 2)),
+        dma((PARTS, ys)),
+        dma((PARTS, ys)),
+        dma((PARTS, 2 * group_size)),
+        dma((PARTS, 2 * group_size)),
         dma,
     ]
     smem = pl.BlockSpec(memory_space=pltpu.SMEM)
@@ -686,7 +743,7 @@
         out_shape=out_shape,
         in_specs=[anywhere] * 4,
         out_specs=[anywhere] * 4,
-        scratch_shapes=[dma((4,))],
+        scratch_shapes=[pltpu.VMEM(shape.shape, LOW) for shape in out_shape] + [dma((2, 4, 4))],
         name="hand_over",
     )(*results)
     return (grad_query[None], grad_hidden[None], grad_key, grad_value)

time: 154 us -> 88 us (0.57)
  Pallas kernels: 154 us -> 87.3 us
    pallas_call x1, Pallas kernels: 66.7 us -> 2.55 us  [on_device(): pl.pallas_call(hand_over, out_shape=out_shape, in_specs=[anywhere] * 4, o...]
    pallas_call x1, Pallas kernels: 87 us -> 84.7 us  [on_device(): pl.pallas_call(kernel, out_shape=out_shape, in_specs=[smem, smem, smem] +...]
where the time goes in v3:
time: 88 us; the launch traced here: 87.9 us
  Pallas kernels  87.3 us (99%)
    pallas_call x1, Pallas kernels, on_device(): pl.pallas_call(kernel, out_shape=out_shape, in_specs=[smem, smem, smem] +...  84.7 us
    pallas_call x1, Pallas kernels, on_device(): pl.pallas_call(hand_over, out_shape=out_shape, in_specs=[anywhere] * 4, o...  2.55 us

profile of v3, /device:TPU:1, one launch (start us, length us, event | category | flops | bytes accessed | tf_op | source)
XLA Modules:
  0.0 87.9 jit_solution(11398749973682939232)
XLA Ops:
  0.6 84.7 %layer.1 = (bf16[128,4096]{1,0:T(8,128)(2,1)}, bf16[128,4096]{1,0:T(8,128)(2,1)}, bf16[32,512]{1,0:T(8,128)(2,1)}, bf16[32,512]{1,0:T(8,128)(2,1)}) custom-call(s32[1,8]{1,0:T(1,128)} %refs_0_.1, s32[1,8]{1,0:T(1,128)} %refs_1_.1, s32[1,8]{1,0:T(1,128)} %refs_2_.1, bf16[128,4096]{1,0:T(8,128)(2,1)} %bitcast.5, bf16[128,4096]{1,0:T(8,128)(2,1)} %bitcast.6, ...), custom_call_target="tpu_custom_call" | custom-call | tf_op jit(solution)/shard_map/layer/pallas_call | solution.py:721
  85.4 2.5 %hand_over.1 = (bf16[128,4096]{1,0:T(8,128)(2,1)}, bf16[128,4096]{1,0:T(8,128)(2,1)}, bf16[32,512]{1,0:T(8,128)(2,1)}, bf16[32,512]{1,0:T(8,128)(2,1)}) custom-call(bf16[128,4096]{1,0:T(8,128)(2,1)} %get-tuple-element.12.refs_0_, bf16[128,4096]{1,0:T(8,128)(2,1)} %get-tuple-element.13.refs_1_, bf16[32,512]{1,0:T(8,128)(2,1)} %get-tuple-element.14.refs_2_, ...), custom_call_target="tpu_custom_call" | custom-call | tf_op jit(solution)/shard_map/hand_over/pallas_call | solution.py:741

commit v4 on v3

--- a/solution.py
+++ b/solution.py
@@ -47,8 +47,7 @@
     hid_v,
     kw_v,
     vw_v,
-    q_r,
-    do_r,
+    qd_r,
     kv_s,
     kv_r,
     kt_v,
@@ -72,11 +71,8 @@
     gh_v,
     begin_v,
     load_sem,
-    own_sem,
-    q_send,
-    q_recv,
-    do_send,
-    do_recv,
+    in_send,
+    in_recv,
     kv_send,
     kv_recv,
     hid_send,
@@ -176,9 +172,9 @@
         at = rows_of(me if to else origin(o))
         return pltpu.make_async_remote_copy(
             src_ref=queries.at[:, cols(first_col(dest) + h * HD, HD)],
-            dst_ref=q_r.at[h, at, :],
-            send_sem=q_send.at[h, o],
-            recv_sem=q_recv.at[h, o],
+            dst_ref=qd_r.at[h, 0, at, :],
+            send_sem=in_send,
+            recv_sem=in_recv.at[h],
             device_id={"grp": dest},
             device_id_type=MESH,
         )
@@ -188,9 +184,9 @@
         at = rows_of(me if to else origin(o))
         return pltpu.make_async_remote_copy(
             src_ref=out_grad.at[:, cols(first_col(dest) + h * HD, HD)],
-            dst_ref=do_r.at[h, at, :],
-            send_sem=do_send.at[h, o],
-            recv_sem=do_recv.at[h, o],
+            dst_ref=qd_r.at[h, 1, at, :],
+            send_sem=in_send,
+            recv_sem=in_recv.at[h],
             device_id={"grp": dest},
             device_id_type=MESH,
         )
@@ -201,8 +197,8 @@
         return pltpu.make_async_remote_copy(
             src_ref=kv_s.at[lax.rem(dest, KVH)],
             dst_ref=kv_r.at[:, at, :],
-            send_sem=kv_send.at[o],
-            recv_sem=kv_recv.at[o],
+            send_sem=kv_send,
+            recv_sem=kv_recv,
             device_id={"grp": dest},
             device_id_type=MESH,
         )
@@ -213,8 +209,8 @@
         return pltpu.make_async_remote_copy(
             src_ref=hid_s.at[dest_y * 2 + dest_core],
             dst_ref=hid_t.at[from_y, :, cols(from_core * rows, rows)],
-            send_sem=hid_send.at[o],
-            recv_sem=hid_recv.at[o],
+            send_sem=hid_send,
+            recv_sem=hid_recv,
             device_id={"dp": column_peer(o)},
             device_id_type=MESH,
         )
@@ -225,8 +221,8 @@
         return pltpu.make_async_remote_copy(
             src_ref=dq_g.at[h, rows_of(dest), :],
             dst_ref=grad_query.at[:, cols(at, HD)],
-            send_sem=dq_send.at[h, o],
-            recv_sem=dq_recv.at[h, o],
+            send_sem=dq_send,
+            recv_sem=dq_recv,
             device_id={"grp": dest},
             device_id_type=MESH,
         )
@@ -235,15 +231,15 @@
         return pltpu.make_async_copy(
             dq_g.at[h, rows_of(me), :],
             grad_query.at[:, cols(first_col(me) + h * HD, HD)],
-            dq_own.at[h],
+            dq_own,
         )
 
     def dl_copy(dest, source):
         return pltpu.make_async_remote_copy(
             src_ref=dl_s.at[dest],
             dst_ref=dl_r.at[source],
-            send_sem=dl_send.at[dest],
-            recv_sem=dl_recv.at[source],
+            send_sem=dl_send,
+            recv_sem=dl_recv,
             device_id={"grp": dest},
             device_id_type=MESH,
         )
@@ -253,8 +249,8 @@
         return pltpu.make_async_remote_copy(
             src_ref=dg_s.at[dest],
             dst_ref=dg_r.at[me if to else origin(o)],
-            send_sem=dg_send.at[o],
-            recv_sem=dg_recv.at[o],
+            send_sem=dg_send,
+            recv_sem=dg_recv,
             device_id={"grp": dest},
             device_id_type=MESH,
         )
@@ -265,7 +261,7 @@
         return pltpu.make_async_remote_copy(
             src_ref=dkv_all.at[y * 2 + core, part],
             dst_ref=dkv_all.at[at, part],
-            send_sem=ya_send.at[part, k],
+            send_sem=ya_send,
             recv_sem=ya_recv.at[part, k],
             device_id={"dp": place(lax.rem(y + step, ys), x_hi, core)},
             device_id_type=MESH,
@@ -279,8 +275,8 @@
         return pltpu.make_async_remote_copy(
             src_ref=dkv_all.at[come, part, half],
             dst_ref=dkv_all.at[come if to else far, part, half],
-            send_sem=yf_send.at[part, k],
-            recv_sem=yf_recv.at[part, k],
+            send_sem=yf_send,
+            recv_sem=yf_recv.at[part],
             device_id={"dp": place(lax.rem(y + step, ys), x_hi, core)},
             device_id_type=MESH,
         )
@@ -290,7 +286,7 @@
         return pltpu.make_async_remote_copy(
             src_ref=dkv_all.at[from_y * 2 + core, part],
             dst_ref=dkv_all.at[from_y * 2 + (core if to else 1 - core), part],
-            send_sem=yc_send.at[part, k],
+            send_sem=yc_send,
             recv_sem=yc_recv.at[part, k],
             device_id={"dp": place(y, x_hi, 1 - core)},
             device_id_type=MESH,
@@ -302,24 +298,30 @@
         return pltpu.make_async_remote_copy(
             src_ref=prod_s.at[part, pl.ds(pl.multiple_of(at * piece, piece), piece), :],
             dst_ref=rs_r.at[part, o],
-            send_sem=rs_send.at[part, o],
-            recv_sem=rs_recv.at[part, o],
+            send_sem=rs_send,
+            recv_sem=rs_recv.at[part],
             device_id=dest,
             device_id_type=MESH,
         )
+
+    def settle(ref, sem):
+        pltpu.make_async_copy(ref, ref, sem).wait()
+
+    others = total - rows
+    seven = pl.ds(0, group_size - 1)
 
     def own_q(h):
         return pltpu.make_async_copy(
             queries.at[:, cols(first_col(me) + h * HD, HD)],
-            q_r.at[h, rows_of(me), :],
-            own_sem.at[0, h],
+            qd_r.at[h, 0, rows_of(me), :],
+            in_recv.at[h],
         )
 
     def own_do(h):
         return pltpu.make_async_copy(
             out_grad.at[:, cols(first_col(me) + h * HD, HD)],
-            do_r.at[h, rows_of(me), :],
-            own_sem.at[1, h],
+            qd_r.at[h, 1, rows_of(me), :],
+            in_recv.at[h],
         )
 
     def send_heads(first, last):
@@ -399,7 +401,7 @@
     sources = [source_block(b * rows) for b in range(group_size)]
 
     acc[...] = jnp.zeros_like(acc)
-    each(1, group_size, lambda o: kv_copy(o, False).wait_recv())
+    settle(kv_r.at[:, pl.ds(0, others), :], kv_recv)
     kt_v[...] = kv_r[0].T
 
     key_ids = lax.broadcasted_iota(jnp.int32, (HD, QBLK), 0)
@@ -412,8 +414,8 @@
         r0 = b * QBLK
         keys = r0 + QBLK
         tiles = keys // HD
-        q_blk = q_r[h, r0 : r0 + QBLK, :]
-        do_blk = do_r[h, r0 : r0 + QBLK, :]
+        q_blk = qd_r[h, 0, r0 : r0 + QBLK, :]
+        do_blk = qd_r[h, 1, r0 : r0 + QBLK, :]
         begin_row = begin_v[:, r0 : r0 + QBLK]
         s_v[0:keys, :] = lax.dot_general(
             kv_r[0, 0:keys, :], q_blk, NT, preferred_element_type=FULL
@@ -462,14 +464,7 @@
         dq_stay(h).start()
 
     def one_head(h):
-        own_q(h).wait()
-        own_do(h).wait()
-
-        def arrive(o):
-            q_copy(h, o, False).wait_recv()
-            do_copy(h, o, False).wait_recv()
-
-        each(1, group_size, arrive)
+        settle(qd_r.at[h], in_recv.at[h])
 
         for b in reversed(range(blocks)):
             attend(h, b)
@@ -496,11 +491,7 @@
     each(0, heads, send_dq)
 
     dl_r[me] = dl_s[me]
-    for s in range(group_size):
-
-        @pl.when(me != s)
-        def _():
-            dl_copy(s, s).wait_recv()
+    settle(dl_r.at[seven], dl_recv)
 
     def merge(received, part, g):
         return (
@@ -516,15 +507,11 @@
             ya_copy(part, k, True).start()
         yc_copy(part, 0, True).start()
 
-    def close_early(o):
-        kv_copy(o, True).wait_send()
-        for h in range(heads):
-            q_copy(h, o, True).wait_send()
-            do_copy(h, o, True).wait_send()
-
-    each(1, group_size, close_early)
-
-    each(1, column, lambda o: hid_copy(o, False).wait_recv())
+    settle(kv_r.at[:, pl.ds(0, others), :], kv_send)
+    settle(qd_r.at[:, :, pl.ds(0, others), :], in_send)
+    settle(hid_s.at[pl.ds(0, column - 1)], hid_send)
+
+    settle(hid_s.at[pl.ds(0, column - 1)], hid_recv)
     def pass_on(part):
         for k in range(2):
             ya_copy(part, k, False).wait_recv()
@@ -532,8 +519,7 @@
             yc_copy(part, 1 if k else ys - 1, True).start()
 
     def hand_far(part):
-        for k in range(2):
-            yf_copy(part, k, False).wait_recv()
+        settle(dkv_all.at[0, part], yf_recv.at[part])
         yc_copy(part, 2, True).start()
 
     def multiply(part):
@@ -557,7 +543,7 @@
         multiply(part)
 
     dg_r[me] = dg_s[me]
-    each(1, group_size, lambda o: dg_copy(o, False).wait_recv())
+    settle(dg_r.at[seven], dg_recv)
     dk_rows = jnp.concatenate([merge(dg_r, 0, g) for g in range(KVH)], axis=1)
     dv_rows = jnp.concatenate([merge(dg_r, 1, g) for g in range(KVH)], axis=1)
 
@@ -572,33 +558,19 @@
     gh_out = pltpu.make_async_copy(gh_v, grad_hidden, gh_sem)
     gh_out.start()
 
-    def close(o):
-        dg_copy(o, True).wait_send()
-        for h in range(heads):
-            dq_copy(h, o, True).wait_send()
-            dq_copy(h, o, False).wait_recv()
-
-    each(1, group_size, close)
-    each(1, column, lambda o: hid_copy(o, True).wait_send())
-    for s in range(group_size):
-
-        @pl.when(me != s)
-        def _():
-            dl_copy(s, me).wait_send()
-
-    for h in range(heads):
-        dq_stay(h).wait()
-    for part in range(PARTS):
-        for k in range(2):
-            ya_copy(part, k, True).wait_send()
-            yf_copy(part, k, True).wait_send()
-        for k in range(ys):
-            yc_copy(part, k, True).wait_send()
+    settle(dg_s.at[seven], dg_send)
+    settle(dl_s.at[seven], dl_send)
+    settle(dq_g.at[:, pl.ds(0, others), :], dq_send)
+    settle(dq_g.at[:, pl.ds(0, others), :], dq_recv)
+    settle(dq_g.at[:, pl.ds(0, rows), :], dq_own)
+    settle(dkv_all.at[pl.ds(0, 2)], ya_send)
+    settle(dkv_all.at[0], yf_send)
+    settle(dkv_all.at[pl.ds(0, ys)], yc_send)
 
     norm = 1.0 / math.sqrt(total * replica_count)
     own = pl.ds(pl.multiple_of((me * 2 + x_hi) * piece, piece), piece)
     for part in range(PARTS):
-        each(1, summed_over, lambda o: rs_copy(part, o).wait_recv())
+        settle(rs_r.at[part, pl.ds(0, summed_over - 1)], rs_recv.at[part])
         summed = prod[part, own, :]
         for o in range(1, summed_over):
             summed = summed + rs_r[part, o].astype(FULL)
@@ -607,8 +579,7 @@
         result[:, at : at + PCOLS] = (summed * norm).astype(LOW)
 
     gh_out.wait()
-    for part in range(PARTS):
-        each(1, summed_over, lambda o: rs_copy(part, o).wait_send())
+    settle(rs_r.at[:, pl.ds(0, summed_over - 1)], rs_send)
 
 
 def hand_over(*refs):
@@ -654,8 +625,7 @@
         pltpu.VMEM((rows, width), LOW),
         pltpu.VMEM((width, kvw), LOW),
         pltpu.VMEM((width, kvw), LOW),
-        pltpu.VMEM((heads, total, HD), LOW),
-        pltpu.VMEM((heads, total, HD), LOW),
+        pltpu.VMEM((heads, 2, total, HD), LOW),
         pltpu.VMEM((KVH, 2, rows, HD), LOW),
         pltpu.VMEM((2, total, HD), LOW),
         pltpu.VMEM((HD, total), LOW),
@@ -679,30 +649,27 @@
         pltpu.VMEM((rows, width), LOW),
         pltpu.VMEM((1, total), jnp.int32),
         dma((3,)),
-        dma((2, heads)),
-        dma((heads, group_size)),
-        dma((heads, group_size)),
-        dma((heads, group_size)),
-        dma((heads, group_size)),
-        dma((group_size,)),
-        dma((group_size,)),
-        dma((column,)),
-        dma((column,)),
-        dma((heads, group_size)),
-        dma((heads, group_size)),
+        dma,
         dma((heads,)),
-        dma((group_size,)),
-        dma((group_size,)),
-        dma((group_size,)),
-        dma((group_size,)),
+        dma,
+        dma,
+        dma,
+        dma,
+        dma,
+        dma,
+        dma,
+        dma,
+        dma,
+        dma,
+        dma,
+        dma,
         dma((PARTS, 2)),
-        dma((PARTS, 2)),
-        dma((PARTS, 2)),
-        dma((PARTS, 2)),
+        dma,
+        dma((PARTS,)),
+        dma,
         dma((PARTS, ys)),
-        dma((PARTS, ys)),
-        dma((PARTS, 2 * group_size)),
-        dma((PARTS, 2 * group_size)),
+        dma,
+        dma((PARTS,)),
         dma,
     ]
     smem = pl.BlockSpec(memory_space=pltpu.SMEM)

time: 88 us -> 84 us (0.955)
  Pallas kernels: 87.3 us -> 83.2 us
    pallas_call x1, Pallas kernels: 84.7 us -> 80.7 us  [on_device(): pl.pallas_call(kernel, out_shape=out_shape, in_specs=[smem, smem, smem] +...]
where the time goes in v4:
time: 84 us; the launch traced here: 83.9 us
  Pallas kernels  83.2 us (99%)
    pallas_call x1, Pallas kernels, on_device(): pl.pallas_call(kernel, out_shape=out_shape, in_specs=[smem, smem, smem] +...  80.7 us
    pallas_call x1, Pallas kernels, on_device(): pl.pallas_call(hand_over, out_shape=out_shape, in_specs=[anywhere] * 4, o...  2.55 us

profile of v4, /device:TPU:1, one launch (start us, length us, event | category | flops | bytes accessed | tf_op | source)
XLA Modules:
  0.0 83.9 jit_solution(8447883351323687909)
XLA Ops:
  0.6 80.7 %layer.1 = (bf16[128,4096]{1,0:T(8,128)(2,1)}, bf16[128,4096]{1,0:T(8,128)(2,1)}, bf16[32,512]{1,0:T(8,128)(2,1)}, bf16[32,512]{1,0:T(8,128)(2,1)}) custom-call(s32[1,8]{1,0:T(1,128)} %refs_0_.1, s32[1,8]{1,0:T(1,128)} %refs_1_.1, s32[1,8]{1,0:T(1,128)} %refs_2_.1, bf16[128,4096]{1,0:T(8,128)(2,1)} %bitcast.5, bf16[128,4096]{1,0:T(8,128)(2,1)} %bitcast.6, ...), custom_call_target="tpu_custom_call" | custom-call | tf_op jit(solution)/shard_map/layer/pallas_call | solution.py:688
  81.3 2.5 %hand_over.1 = (bf16[128,4096]{1,0:T(8,128)(2,1)}, bf16[128,4096]{1,0:T(8,128)(2,1)}, bf16[32,512]{1,0:T(8,128)(2,1)}, bf16[32,512]{1,0:T(8,128)(2,1)}) custom-call(bf16[128,4096]{1,0:T(8,128)(2,1)} %get-tuple-element.12.refs_0_, bf16[128,4096]{1,0:T(8,128)(2,1)} %get-tuple-element.13.refs_1_, bf16[32,512]{1,0:T(8,128)(2,1)} %get-tuple-element.14.refs_2_, ...), custom_call_target="tpu_custom_call" | custom-call | tf_op jit(solution)/shard_map/hand_over/pallas_call | solution.py:708

commit v5 on v4

--- a/solution.py
+++ b/solution.py
@@ -174,7 +174,7 @@
             src_ref=queries.at[:, cols(first_col(dest) + h * HD, HD)],
             dst_ref=qd_r.at[h, 0, at, :],
             send_sem=in_send,
-            recv_sem=in_recv.at[h],
+            recv_sem=in_recv.at[h, 0],
             device_id={"grp": dest},
             device_id_type=MESH,
         )
@@ -186,7 +186,7 @@
             src_ref=out_grad.at[:, cols(first_col(dest) + h * HD, HD)],
             dst_ref=qd_r.at[h, 1, at, :],
             send_sem=in_send,
-            recv_sem=in_recv.at[h],
+            recv_sem=in_recv.at[h, 1],
             device_id={"grp": dest},
             device_id_type=MESH,
         )
@@ -234,12 +234,12 @@
             dq_own,
         )
 
-    def dl_copy(dest, source):
-        return pltpu.make_async_remote_copy(
-            src_ref=dl_s.at[dest],
-            dst_ref=dl_r.at[source],
+    def dl_copy(part, dest):
+        return pltpu.make_async_remote_copy(
+            src_ref=dl_s.at[dest, part],
+            dst_ref=dl_r.at[me, part],
             send_sem=dl_send,
-            recv_sem=dl_recv,
+            recv_sem=dl_recv.at[part],
             device_id={"grp": dest},
             device_id_type=MESH,
         )
@@ -256,7 +256,7 @@
         )
 
     def ya_copy(part, k, to):
-        step = ys - 1 if k else 1
+        step = (1, ys - 1, 2)[k]
         at = (y if to else lax.rem(y + ys - step, ys)) * 2 + core
         return pltpu.make_async_remote_copy(
             src_ref=dkv_all.at[y * 2 + core, part],
@@ -314,24 +314,19 @@
         return pltpu.make_async_copy(
             queries.at[:, cols(first_col(me) + h * HD, HD)],
             qd_r.at[h, 0, rows_of(me), :],
-            in_recv.at[h],
+            in_recv.at[h, 0],
         )
 
     def own_do(h):
         return pltpu.make_async_copy(
             out_grad.at[:, cols(first_col(me) + h * HD, HD)],
             qd_r.at[h, 1, rows_of(me), :],
-            in_recv.at[h],
-        )
-
-    def send_heads(first, last):
-        def one(i):
-            h = i // (group_size - 1)
-            o = lax.rem(i, group_size - 1) + 1
-            q_copy(h, o, True).start()
-            do_copy(h, o, True).start()
-
-        each(first * (group_size - 1), last * (group_size - 1), one)
+            in_recv.at[h, 1],
+        )
+
+    def send_head(h):
+        each(1, group_size, lambda o: q_copy(h, o, True).start())
+        each(1, group_size, lambda o: do_copy(h, o, True).start())
 
     load_hid.wait()
     load_kw.wait()
@@ -352,7 +347,7 @@
     pl.semaphore_wait(barrier, column - 1 + summed_over - 1)
 
     each(1, group_size, lambda o: kv_copy(o, True).start())
-    send_heads(0, heads)
+    each(0, heads, send_head)
     for h in range(heads):
         own_q(h).start()
         own_do(h).start()
@@ -410,22 +405,21 @@
     def fold(tile):
         return tile.reshape(HD // 8, 8, QBLK)
 
-    def attend(h, b):
+    def span(b):
+        first = sum((i + 1) * QBLK for i in range(b))
+        return first, (b + 1) * QBLK
+
+    def weigh(h, b):
         r0 = b * QBLK
-        keys = r0 + QBLK
-        tiles = keys // HD
+        first, keys = span(b)
         q_blk = qd_r[h, 0, r0 : r0 + QBLK, :]
-        do_blk = qd_r[h, 1, r0 : r0 + QBLK, :]
         begin_row = begin_v[:, r0 : r0 + QBLK]
-        s_v[0:keys, :] = lax.dot_general(
+        s_v[first : first + keys, :] = lax.dot_general(
             kv_r[0, 0:keys, :], q_blk, NT, preferred_element_type=FULL
         )
-        pg_v[0:keys, :] = lax.dot_general(
-            kv_r[1, 0:keys, :], do_blk, NT, preferred_element_type=FULL
-        )
         top = jnp.full((8, QBLK), -1e30, FULL)
-        for j in range(tiles):
-            at = slice(j * HD, (j + 1) * HD)
+        for j in range(keys // HD):
+            at = slice(first + j * HD, first + (j + 1) * HD)
             seen = key_ids + j * HD >= begin_row
             if j * HD >= r0:
                 seen = seen & (key_ids + (j * HD - r0) <= lane_ids)
@@ -434,27 +428,38 @@
             top = jnp.maximum(top, jnp.max(fold(tile), axis=0))
         top = jnp.max(top, axis=0, keepdims=True)
         mass = jnp.zeros((8, QBLK), FULL)
-        for j in range(tiles):
-            at = slice(j * HD, (j + 1) * HD)
+        for j in range(keys // HD):
+            at = slice(first + j * HD, first + (j + 1) * HD)
             tile = jnp.exp2((s_v[at, :] - top) * exp_scale)
             s_v[at, :] = tile
             mass = mass + jnp.sum(fold(tile), axis=0)
         inverse = 1.0 / jnp.sum(mass, axis=0, keepdims=True)
+        for j in range(keys // HD):
+            at = slice(first + j * HD, first + (j + 1) * HD)
+            weights = s_v[at, :] * inverse
+            s_v[at, :] = weights
+            wl_v[at, :] = weights.astype(LOW)
+
+    def attend(h, b):
+        r0 = b * QBLK
+        first, keys = span(b)
+        q_blk = qd_r[h, 0, r0 : r0 + QBLK, :]
+        do_blk = qd_r[h, 1, r0 : r0 + QBLK, :]
+        pg_v[first : first + keys, :] = lax.dot_general(
+            kv_r[1, 0:keys, :], do_blk, NT, preferred_element_type=FULL
+        )
         delta = jnp.zeros((8, QBLK), FULL)
-        for j in range(tiles):
-            at = slice(j * HD, (j + 1) * HD)
-            weights = s_v[at, :] * inverse
-            low = weights.astype(LOW)
-            s_v[at, :] = weights
-            wl_v[at, :] = low
-            delta = delta + jnp.sum(fold(low.astype(FULL) * pg_v[at, :]), axis=0)
+        for j in range(keys // HD):
+            at = slice(first + j * HD, first + (j + 1) * HD)
+            delta = delta + jnp.sum(fold(wl_v[at, :].astype(FULL) * pg_v[at, :]), axis=0)
         delta = jnp.sum(delta, axis=0, keepdims=True)
-        for j in range(tiles):
-            at = slice(j * HD, (j + 1) * HD)
+        for j in range(keys // HD):
+            at = slice(first + j * HD, first + (j + 1) * HD)
             ds_v[at, :] = (s_v[at, :] * (pg_v[at, :] - delta)).astype(LOW)
-        acc[1, 0:keys, :] += jnp.dot(wl_v[0:keys, :], do_blk, preferred_element_type=FULL)
-        acc[0, 0:keys, :] += jnp.dot(ds_v[0:keys, :], q_blk, preferred_element_type=FULL)
-        grad_t = jnp.dot(kt_v[:, 0:keys], ds_v[0:keys, :], preferred_element_type=FULL)
+        all_keys = slice(first, first + keys)
+        acc[1, 0:keys, :] += jnp.dot(wl_v[all_keys, :], do_blk, preferred_element_type=FULL)
+        acc[0, 0:keys, :] += jnp.dot(ds_v[all_keys, :], q_blk, preferred_element_type=FULL)
+        grad_t = jnp.dot(kt_v[:, 0:keys], ds_v[all_keys, :], preferred_element_type=FULL)
         grad_rows = (grad_t * inv_root).T.astype(LOW)
         for j in range(per_block):
             dq_s[r0 // rows + j] = grad_rows[j * rows : (j + 1) * rows, :]
@@ -464,34 +469,41 @@
         dq_stay(h).start()
 
     def one_head(h):
-        settle(qd_r.at[h], in_recv.at[h])
+        settle(qd_r.at[h, 0], in_recv.at[h, 0])
+        for b in reversed(range(blocks)):
+            weigh(h, b)
+        settle(qd_r.at[h, 1], in_recv.at[h, 1])
+
+        @pl.when(h == heads - 1)
+        def _():
+            send_dq(0)
 
         for b in reversed(range(blocks)):
             attend(h, b)
 
             @pl.when(h == heads - 1)
             def _():
-                for j in range(b * per_block, (b + 1) * per_block):
-                    at = slice(j * rows, (j + 1) * rows)
-                    dl_s[j, 0] = (acc[0, at, :] * inv_root).astype(LOW)
-                    dl_s[j, 1] = acc[1, at, :].astype(LOW)
-
-                    @pl.when(me != j)
-                    def _():
-                        dl_copy(j, me).start()
+                for part in range(2):
+                    for j in range(b * per_block, (b + 1) * per_block):
+                        at = slice(j * rows, (j + 1) * rows)
+                        term = acc[part, at, :]
+                        if part == 0:
+                            term = term * inv_root
+                        dl_s[j, part] = term.astype(LOW)
+
+                        @pl.when(me != j)
+                        def _():
+                            dl_copy(part, j).start()
 
         for b in range(group_size):
             dq_g[h, b * rows : (b + 1) * rows, :] = dq_s[sources[b]]
 
     each(0, heads, one_head)
 
+    send_dq(1)
+    dl_r[me] = dl_s[me]
     for b in range(group_size):
         dg_s[b] = dl_s[sources[b]]
-    each(1, group_size, lambda o: dg_copy(o, True).start())
-    each(0, heads, send_dq)
-
-    dl_r[me] = dl_s[me]
-    settle(dl_r.at[seven], dl_recv)
 
     def merge(received, part, g):
         return (
@@ -499,14 +511,19 @@
         ).astype(LOW)
 
     for part in range(PARTS):
+        which = part * PCOLS // kvw
+        if part * PCOLS % kvw == 0:
+            settle(dl_r.at[seven, which], dl_recv.at[which])
         for i in range(PCOLS // HD):
             dkv_all[y * 2 + core, part, :, i * HD : (i + 1) * HD] = merge(
-                dl_r, part * PCOLS // kvw, (part * PCOLS % kvw) // HD + i
+                dl_r, which, (part * PCOLS % kvw) // HD + i
             )
-        for k in range(2):
+        for k in range(3 if part == PARTS - 1 else 2):
             ya_copy(part, k, True).start()
         yc_copy(part, 0, True).start()
 
+    each(1, group_size, lambda o: dg_copy(o, True).start())
+    each(2, heads, send_dq)
     settle(kv_r.at[:, pl.ds(0, others), :], kv_send)
     settle(qd_r.at[:, :, pl.ds(0, others), :], in_send)
     settle(hid_s.at[pl.ds(0, column - 1)], hid_send)
@@ -515,11 +532,15 @@
     def pass_on(part):
         for k in range(2):
             ya_copy(part, k, False).wait_recv()
-            yf_copy(part, k, True).start()
+            if part < PARTS - 1:
+                yf_copy(part, k, True).start()
             yc_copy(part, 1 if k else ys - 1, True).start()
 
     def hand_far(part):
-        settle(dkv_all.at[0, part], yf_recv.at[part])
+        if part < PARTS - 1:
+            settle(dkv_all.at[0, part], yf_recv.at[part])
+        else:
+            ya_copy(part, 2, False).wait_recv()
         yc_copy(part, 2, True).start()
 
     def multiply(part):
@@ -564,7 +585,8 @@
     settle(dq_g.at[:, pl.ds(0, others), :], dq_recv)
     settle(dq_g.at[:, pl.ds(0, rows), :], dq_own)
     settle(dkv_all.at[pl.ds(0, 2)], ya_send)
-    settle(dkv_all.at[0], yf_send)
+    settle(dkv_all.at[0, 0], ya_send)
+    settle(dkv_all.at[0, pl.ds(0, PARTS - 1)], yf_send)
     settle(dkv_all.at[pl.ds(0, ys)], yc_send)
 
     norm = 1.0 / math.sqrt(total * replica_count)
@@ -620,6 +642,7 @@
     ys = replica_count // 4
     column = 2 * ys
     chunk = width // column
+    tall = sum((b + 1) * QBLK for b in range(blocks))
     dma = pltpu.SemaphoreType.DMA
     scratch = [
         pltpu.VMEM((rows, width), LOW),
@@ -631,10 +654,10 @@
         pltpu.VMEM((HD, total), LOW),
         pltpu.VMEM((column, chunk, rows), LOW),
         pltpu.VMEM((ys, chunk, 2 * rows), LOW),
-        pltpu.VMEM((total, QBLK), FULL),
-        pltpu.VMEM((total, QBLK), FULL),
-        pltpu.VMEM((total, QBLK), LOW),
-        pltpu.VMEM((total, QBLK), LOW),
+        pltpu.VMEM((tall, QBLK), FULL),
+        pltpu.VMEM((tall, QBLK), FULL),
+        pltpu.VMEM((tall, QBLK), LOW),
+        pltpu.VMEM((tall, QBLK), LOW),
         pltpu.VMEM((2, total, HD), FULL),
         pltpu.VMEM((group_size, rows, HD), LOW),
         pltpu.VMEM((heads, total, HD), LOW),
@@ -650,22 +673,22 @@
         pltpu.VMEM((1, total), jnp.int32),
         dma((3,)),
         dma,
-        dma((heads,)),
-        dma,
-        dma,
-        dma,
-        dma,
-        dma,
-        dma,
-        dma,
-        dma,
-        dma,
-        dma,
-        dma,
-        dma,
-        dma((PARTS, 2)),
-        dma,
-        dma((PARTS,)),
+        dma((heads, 2)),
+        dma,
+        dma,
+        dma,
+        dma,
+        dma,
+        dma,
+        dma,
+        dma,
+        dma((2,)),
+        dma,
+        dma,
+        dma,
+        dma((PARTS, 3)),
+        dma,
+        dma((PARTS - 1,)),
         dma,
         dma((PARTS, ys)),
         dma,

time: 84 us -> 82.9 us (0.987)
  Pallas kernels: 83.2 us -> 82.1 us
    pallas_call x1, Pallas kernels: 80.7 us -> 79.5 us  [on_device(): pl.pallas_call(kernel, out_shape=out_shape, in_specs=[smem, smem, smem] +...]
where the time goes in v5:
time: 82.9 us; the launch traced here: 82.7 us
  Pallas kernels  82.1 us (99%)
    pallas_call x1, Pallas kernels, on_device(): pl.pallas_call(kernel, out_shape=out_shape, in_specs=[smem, smem, smem] +...  79.5 us
    pallas_call x1, Pallas kernels, on_device(): pl.pallas_call(hand_over, out_shape=out_shape, in_specs=[anywhere] * 4, o...  2.55 us

profile of v5, /device:TPU:1, one launch (start us, length us, event | category | flops | bytes accessed | tf_op | source)
XLA Modules:
  0.0 82.7 jit_solution(8634193118209991212)
XLA Ops:
  0.6 79.5 %layer.1 = (bf16[128,4096]{1,0:T(8,128)(2,1)}, bf16[128,4096]{1,0:T(8,128)(2,1)}, bf16[32,512]{1,0:T(8,128)(2,1)}, bf16[32,512]{1,0:T(8,128)(2,1)}) custom-call(s32[1,8]{1,0:T(1,128)} %refs_0_.1, s32[1,8]{1,0:T(1,128)} %refs_1_.1, s32[1,8]{1,0:T(1,128)} %refs_2_.1, bf16[128,4096]{1,0:T(8,128)(2,1)} %bitcast.5, bf16[128,4096]{1,0:T(8,128)(2,1)} %bitcast.6, ...), custom_call_target="tpu_custom_call" | custom-call | tf_op jit(solution)/shard_map/layer/pallas_call | solution.py:711
  80.2 2.5 %hand_over.1 = (bf16[128,4096]{1,0:T(8,128)(2,1)}, bf16[128,4096]{1,0:T(8,128)(2,1)}, bf16[32,512]{1,0:T(8,128)(2,1)}, bf16[32,512]{1,0:T(8,128)(2,1)}) custom-call(bf16[128,4096]{1,0:T(8,128)(2,1)} %get-tuple-element.12.refs_0_, bf16[128,4096]{1,0:T(8,128)(2,1)} %get-tuple-element.13.refs_1_, bf16[32,512]{1,0:T(8,128)(2,1)} %get-tuple-element.14.refs_2_, ...), custom_call_target="tpu_custom_call" | custom-call | tf_op jit(solution)/shard_map/hand_over/pallas_call | solution.py:731

commit v6 on v5

--- a/solution.py
+++ b/solution.py
@@ -66,7 +66,9 @@
     dg_r,
     dkv_all,
     prod,
-    prod_s,
+    rx_s,
+    rx_r,
+    rs_s,
     rs_r,
     gh_v,
     begin_v,
@@ -90,6 +92,8 @@
     yf_recv,
     yc_send,
     yc_recv,
+    rx_send,
+    rx_recv,
     rs_send,
     rs_recv,
     gh_sem,
@@ -100,7 +104,6 @@
     y, x_hi, core = rep // 4, lax.rem(rep // 2, 2), lax.rem(rep, 2)
     ys = replica_count // 4
     column = 2 * ys
-    summed_over = 2 * group_size
     rows = hidden.shape[0]
     width = hidden.shape[1]
     total = rows * group_size
@@ -108,6 +111,7 @@
     wide = heads * HD
     kvw = KVH * HD
     piece = width // (group_size * replica_count)
+    half_rows = group_size * piece
     inv_root = 1.0 / math.sqrt(HD)
     exp_scale = inv_root / math.log(2.0)
     blocks = total // QBLK
@@ -146,11 +150,7 @@
     def column_origin(o):
         return lax.rem(y - o // 2 + ys, ys), lax.rem(core + o, 2)
 
-    def sum_peer(o):
-        return {
-            "grp": peer(lax.rem(o, group_size)),
-            "dp": place(y, lax.rem(x_hi + o // group_size, 2), core),
-        }
+    across = {"grp": lax.rem(me + ZS, group_size), "dp": place(y, 1 - x_hi, core)}
 
     each(
         1,
@@ -161,11 +161,12 @@
     )
     each(
         1,
-        summed_over,
+        group_size,
         lambda o: pl.semaphore_signal(
-            barrier, inc=1, device_id=sum_peer(o), device_id_type=MESH
+            barrier, inc=1, device_id={"grp": peer(o)}, device_id_type=MESH
         ),
     )
+    pl.semaphore_signal(barrier, inc=1, device_id=across, device_id_type=MESH)
 
     def q_copy(h, o, to):
         dest = peer(o)
@@ -292,15 +293,24 @@
             device_id_type=MESH,
         )
 
+    def rx_copy(part):
+        return pltpu.make_async_remote_copy(
+            src_ref=rx_s.at[part],
+            dst_ref=rx_r.at[part],
+            send_sem=rx_send,
+            recv_sem=rx_recv.at[part],
+            device_id=across,
+            device_id_type=MESH,
+        )
+
     def rs_copy(part, o):
-        dest = sum_peer(o)
-        at = dest["grp"] * 2 + lax.rem(x_hi + o // group_size, 2)
-        return pltpu.make_async_remote_copy(
-            src_ref=prod_s.at[part, pl.ds(pl.multiple_of(at * piece, piece), piece), :],
+        dest = peer(o)
+        return pltpu.make_async_remote_copy(
+            src_ref=rs_s.at[part, pl.ds(pl.multiple_of(dest * piece, piece), piece), :],
             dst_ref=rs_r.at[part, o],
             send_sem=rs_send,
             recv_sem=rs_recv.at[part],
-            device_id=dest,
+            device_id={"grp": dest},
             device_id_type=MESH,
         )
 
@@ -344,7 +354,7 @@
     load_vw.wait()
     project(vw_v, 1)
 
-    pl.semaphore_wait(barrier, column - 1 + summed_over - 1)
+    pl.semaphore_wait(barrier, column - 1 + group_size - 1 + 1)
 
     each(1, group_size, lambda o: kv_copy(o, True).start())
     each(0, heads, send_head)
@@ -360,7 +370,7 @@
         g = t // ys
         to_y = lax.rem(t, ys)
         for xh in range(2):
-            at = pl.ds(pl.multiple_of((g * 2 + xh) * piece, piece), piece)
+            at = pl.ds(pl.multiple_of((xh * group_size + g) * piece, piece), piece)
             for c in range(2):
                 hid_s[to_y * 2 + c, at, :] = turned[(xh * 2 + c) * piece :][:piece]
 
@@ -552,9 +562,16 @@
             if k > 0:
                 term = prod[part] + term
             prod[part] = term
-            if k == 2:
-                prod_s[part] = term.astype(LOW)
-        each(1, summed_over, lambda o: rs_copy(part, o).start())
+        rx_s[part] = prod[part, pl.ds((1 - x_hi) * half_rows, half_rows), :].astype(LOW)
+        rx_copy(part).start()
+
+    def combine(part):
+        settle(rx_r.at[part], rx_recv.at[part])
+        at = pl.ds(x_hi * half_rows, half_rows)
+        both = prod[part, at, :] + rx_r[part].astype(FULL)
+        prod[part, at, :] = both
+        rs_s[part] = both.astype(LOW)
+        each(1, group_size, lambda o: rs_copy(part, o).start())
 
     pass_on(0)
     for part in range(PARTS):
@@ -562,6 +579,9 @@
             pass_on(part + 1)
         hand_far(part)
         multiply(part)
+        if part > 0:
+            combine(part - 1)
+    combine(PARTS - 1)
 
     dg_r[me] = dg_s[me]
     settle(dg_r.at[seven], dg_recv)
@@ -590,18 +610,19 @@
     settle(dkv_all.at[pl.ds(0, ys)], yc_send)
 
     norm = 1.0 / math.sqrt(total * replica_count)
-    own = pl.ds(pl.multiple_of((me * 2 + x_hi) * piece, piece), piece)
+    own = pl.ds(pl.multiple_of((x_hi * group_size + me) * piece, piece), piece)
     for part in range(PARTS):
-        settle(rs_r.at[part, pl.ds(0, summed_over - 1)], rs_recv.at[part])
+        settle(rs_r.at[part, seven], rs_recv.at[part])
         summed = prod[part, own, :]
-        for o in range(1, summed_over):
+        for o in range(1, group_size):
             summed = summed + rs_r[part, o].astype(FULL)
         result = grad_value if part * PCOLS >= kvw else grad_key
         at = part * PCOLS % kvw
         result[:, at : at + PCOLS] = (summed * norm).astype(LOW)
 
     gh_out.wait()
-    settle(rs_r.at[:, pl.ds(0, summed_over - 1)], rs_send)
+    settle(rx_r, rx_send)
+    settle(rs_r.at[:, seven], rs_send)
 
 
 def hand_over(*refs):
@@ -667,8 +688,10 @@
         pltpu.VMEM((group_size, 2, rows, HD), LOW),
         pltpu.VMEM((column, PARTS, rows, PCOLS), LOW),
         pltpu.VMEM((PARTS, chunk, PCOLS), FULL),
-        pltpu.VMEM((PARTS, chunk, PCOLS), LOW),
-        pltpu.VMEM((PARTS, 2 * group_size, piece, PCOLS), LOW),
+        pltpu.VMEM((PARTS, chunk // 2, PCOLS), LOW),
+        pltpu.VMEM((PARTS, chunk // 2, PCOLS), LOW),
+        pltpu.VMEM((PARTS, chunk // 2, PCOLS), LOW),
+        pltpu.VMEM((PARTS, group_size, piece, PCOLS), LOW),
         pltpu.VMEM((rows, width), LOW),
         pltpu.VMEM((1, total), jnp.int32),
         dma((3,)),
@@ -691,6 +714,8 @@
         dma((PARTS - 1,)),
         dma,
         dma((PARTS, ys)),
+        dma,
+        dma((PARTS,)),
         dma,
         dma((PARTS,)),
         dma,

time: 82.9 us -> 86.8 us (1.047)
  Pallas kernels: 82.1 us -> 86 us
    pallas_call x1, Pallas kernels: 79.5 us -> 83.5 us  [on_device(): pl.pallas_call(kernel, out_shape=out_shape, in_specs=[smem, smem, smem] +...]
where the time goes in v6:
time: 86.8 us; the launch traced here: 86.6 us
  Pallas kernels  86 us (99%)
    pallas_call x1, Pallas kernels, on_device(): pl.pallas_call(kernel, out_shape=out_shape, in_specs=[smem, smem, smem] +...  83.5 us
    pallas_call x1, Pallas kernels, on_device(): pl.pallas_call(hand_over, out_shape=out_shape, in_specs=[anywhere] * 4, o...  2.55 us

profile of v6, /device:TPU:1, one launch (start us, length us, event | category | flops | bytes accessed | tf_op | source)
XLA Modules:
  0.0 86.6 jit_solution(11611249526533157618)
XLA Ops:
  0.6 83.5 %layer.1 = (bf16[128,4096]{1,0:T(8,128)(2,1)}, bf16[128,4096]{1,0:T(8,128)(2,1)}, bf16[32,512]{1,0:T(8,128)(2,1)}, bf16[32,512]{1,0:T(8,128)(2,1)}) custom-call(s32[1,8]{1,0:T(1,128)} %refs_0_.1, s32[1,8]{1,0:T(1,128)} %refs_1_.1, s32[1,8]{1,0:T(1,128)} %refs_2_.1, bf16[128,4096]{1,0:T(8,128)(2,1)} %bitcast.5, bf16[128,4096]{1,0:T(8,128)(2,1)} %bitcast.6, ...), custom_call_target="tpu_custom_call" | custom-call | tf_op jit(solution)/shard_map/layer/pallas_call | solution.py:736
  84.1 2.5 %hand_over.1 = (bf16[128,4096]{1,0:T(8,128)(2,1)}, bf16[128,4096]{1,0:T(8,128)(2,1)}, bf16[32,512]{1,0:T(8,128)(2,1)}, bf16[32,512]{1,0:T(8,128)(2,1)}) custom-call(bf16[128,4096]{1,0:T(8,128)(2,1)} %get-tuple-element.12.refs_0_, bf16[128,4096]{1,0:T(8,128)(2,1)} %get-tuple-element.13.refs_1_, bf16[32,512]{1,0:T(8,128)(2,1)} %get-tuple-element.14.refs_2_, ...), custom_call_target="tpu_custom_call" | custom-call | tf_op jit(solution)/shard_map/hand_over/pallas_call | solution.py:756

commit v7 on v5

--- a/solution.py
+++ b/solution.py
@@ -70,6 +70,7 @@
     rs_r,
     gh_v,
     begin_v,
+    inv_v,
     load_sem,
     in_send,
     in_recv,
@@ -328,6 +329,9 @@
         each(1, group_size, lambda o: q_copy(h, o, True).start())
         each(1, group_size, lambda o: do_copy(h, o, True).start())
 
+    pl.semaphore_wait(barrier, column - 1 + summed_over - 1)
+    send_head(0)
+
     load_hid.wait()
     load_kw.wait()
     hid_rows = hid_v[...]
@@ -344,10 +348,8 @@
     load_vw.wait()
     project(vw_v, 1)
 
-    pl.semaphore_wait(barrier, column - 1 + summed_over - 1)
-
     each(1, group_size, lambda o: kv_copy(o, True).start())
-    each(0, heads, send_head)
+    each(1, heads, send_head)
     for h in range(heads):
         own_q(h).start()
         own_do(h).start()
@@ -414,18 +416,18 @@
         first, keys = span(b)
         q_blk = qd_r[h, 0, r0 : r0 + QBLK, :]
         begin_row = begin_v[:, r0 : r0 + QBLK]
-        s_v[first : first + keys, :] = lax.dot_general(
-            kv_r[0, 0:keys, :], q_blk, NT, preferred_element_type=FULL
-        )
         top = jnp.full((8, QBLK), -1e30, FULL)
-        for j in range(keys // HD):
-            at = slice(first + j * HD, first + (j + 1) * HD)
-            seen = key_ids + j * HD >= begin_row
-            if j * HD >= r0:
-                seen = seen & (key_ids + (j * HD - r0) <= lane_ids)
-            tile = jnp.where(seen, s_v[at, :], -1e30)
-            s_v[at, :] = tile
-            top = jnp.maximum(top, jnp.max(fold(tile), axis=0))
+        for j in range(0, keys, QBLK):
+            block = lax.dot_general(
+                kv_r[0, j : j + QBLK, :], q_blk, NT, preferred_element_type=FULL
+            )
+            for i in range(j, j + QBLK, HD):
+                seen = key_ids + i >= begin_row
+                if j >= r0:
+                    seen = seen & (key_ids + (i - r0) <= lane_ids)
+                tile = jnp.where(seen, block[i - j : i - j + HD], -1e30)
+                s_v[first + i : first + i + HD, :] = tile
+                top = jnp.maximum(top, jnp.max(fold(tile), axis=0))
         top = jnp.max(top, axis=0, keepdims=True)
         mass = jnp.zeros((8, QBLK), FULL)
         for j in range(keys // HD):
@@ -434,32 +436,40 @@
             s_v[at, :] = tile
             mass = mass + jnp.sum(fold(tile), axis=0)
         inverse = 1.0 / jnp.sum(mass, axis=0, keepdims=True)
+        inv_v[b : b + 1, :] = inverse
         for j in range(keys // HD):
             at = slice(first + j * HD, first + (j + 1) * HD)
-            weights = s_v[at, :] * inverse
-            s_v[at, :] = weights
-            wl_v[at, :] = weights.astype(LOW)
+            wl_v[at, :] = (s_v[at, :] * inverse).astype(LOW)
 
     def attend(h, b):
         r0 = b * QBLK
         first, keys = span(b)
         q_blk = qd_r[h, 0, r0 : r0 + QBLK, :]
         do_blk = qd_r[h, 1, r0 : r0 + QBLK, :]
-        pg_v[first : first + keys, :] = lax.dot_general(
-            kv_r[1, 0:keys, :], do_blk, NT, preferred_element_type=FULL
-        )
         delta = jnp.zeros((8, QBLK), FULL)
+        for j in range(0, keys, QBLK):
+            at = slice(first + j, first + j + QBLK)
+            block = lax.dot_general(
+                kv_r[1, j : j + QBLK, :], do_blk, NT, preferred_element_type=FULL
+            )
+            pg_v[at, :] = block
+            terms = wl_v[at, :].astype(FULL) * block
+            delta = delta + jnp.sum(terms.reshape(QBLK // 8, 8, QBLK), axis=0)
+        delta = jnp.sum(delta, axis=0, keepdims=True)
+        inverse = inv_v[b : b + 1, :]
         for j in range(keys // HD):
             at = slice(first + j * HD, first + (j + 1) * HD)
-            delta = delta + jnp.sum(fold(wl_v[at, :].astype(FULL) * pg_v[at, :]), axis=0)
-        delta = jnp.sum(delta, axis=0, keepdims=True)
-        for j in range(keys // HD):
-            at = slice(first + j * HD, first + (j + 1) * HD)
-            ds_v[at, :] = (s_v[at, :] * (pg_v[at, :] - delta)).astype(LOW)
+            ds_v[at, :] = (s_v[at, :] * inverse * (pg_v[at, :] - delta)).astype(LOW)
         all_keys = slice(first, first + keys)
         acc[1, 0:keys, :] += jnp.dot(wl_v[all_keys, :], do_blk, preferred_element_type=FULL)
         acc[0, 0:keys, :] += jnp.dot(ds_v[all_keys, :], q_blk, preferred_element_type=FULL)
-        grad_t = jnp.dot(kt_v[:, 0:keys], ds_v[all_keys, :], preferred_element_type=FULL)
+
+    def query_grad(b):
+        r0 = b * QBLK
+        first, keys = span(b)
+        grad_t = jnp.dot(
+            kt_v[:, 0:keys], ds_v[first : first + keys, :], preferred_element_type=FULL
+        )
         grad_rows = (grad_t * inv_root).T.astype(LOW)
         for j in range(per_block):
             dq_s[r0 // rows + j] = grad_rows[j * rows : (j + 1) * rows, :]
@@ -495,12 +505,13 @@
                         def _():
                             dl_copy(part, j).start()
 
+        for b in range(blocks):
+            query_grad(b)
         for b in range(group_size):
             dq_g[h, b * rows : (b + 1) * rows, :] = dq_s[sources[b]]
 
     each(0, heads, one_head)
 
-    send_dq(1)
     dl_r[me] = dl_s[me]
     for b in range(group_size):
         dg_s[b] = dl_s[sources[b]]
@@ -523,7 +534,7 @@
         yc_copy(part, 0, True).start()
 
     each(1, group_size, lambda o: dg_copy(o, True).start())
-    each(2, heads, send_dq)
+    each(1, heads, send_dq)
     settle(kv_r.at[:, pl.ds(0, others), :], kv_send)
     settle(qd_r.at[:, :, pl.ds(0, others), :], in_send)
     settle(hid_s.at[pl.ds(0, column - 1)], hid_send)
@@ -671,6 +682,7 @@
         pltpu.VMEM((PARTS, 2 * group_size, piece, PCOLS), LOW),
         pltpu.VMEM((rows, width), LOW),
         pltpu.VMEM((1, total), jnp.int32),
+        pltpu.VMEM((8, QBLK), FULL),
         dma((3,)),
         dma,
         dma((heads, 2)),

time: 82.9 us -> 83 us (level)
  no operation moved by 1% of the time
where the time goes in v7:
time: 83 us; the launch traced here: 82.7 us
  Pallas kernels  82.1 us (99%)
    pallas_call x1, Pallas kernels, on_device(): pl.pallas_call(kernel, out_shape=out_shape, in_specs=[smem, smem, smem] +...  79.5 us
    pallas_call x1, Pallas kernels, on_device(): pl.pallas_call(hand_over, out_shape=out_shape, in_specs=[anywhere] * 4, o...  2.55 us

profile of v7, /device:TPU:1, one launch (start us, length us, event | category | flops | bytes accessed | tf_op | source)
XLA Modules:
  0.0 82.7 jit_solution(6933736699278818538)
XLA Ops:
  0.6 79.5 %layer.1 = (bf16[128,4096]{1,0:T(8,128)(2,1)}, bf16[128,4096]{1,0:T(8,128)(2,1)}, bf16[32,512]{1,0:T(8,128)(2,1)}, bf16[32,512]{1,0:T(8,128)(2,1)}) custom-call(s32[1,8]{1,0:T(1,128)} %refs_0_.1, s32[1,8]{1,0:T(1,128)} %refs_1_.1, s32[1,8]{1,0:T(1,128)} %refs_2_.1, bf16[128,4096]{1,0:T(8,128)(2,1)} %bitcast.5, bf16[128,4096]{1,0:T(8,128)(2,1)} %bitcast.6, ...), custom_call_target="tpu_custom_call" | custom-call | tf_op jit(solution)/shard_map/layer/pallas_call | solution.py:723
  80.2 2.5 %hand_over.1 = (bf16[128,4096]{1,0:T(8,128)(2,1)}, bf16[128,4096]{1,0:T(8,128)(2,1)}, bf16[32,512]{1,0:T(8,128)(2,1)}, bf16[32,512]{1,0:T(8,128)(2,1)}) custom-call(bf16[128,4096]{1,0:T(8,128)(2,1)} %get-tuple-element.12.refs_0_, bf16[128,4096]{1,0:T(8,128)(2,1)} %get-tuple-element.13.refs_1_, bf16[32,512]{1,0:T(8,128)(2,1)} %get-tuple-element.14.refs_2_, ...), custom_call_target="tpu_custom_call" | custom-call | tf_op jit(solution)/shard_map/hand_over/pallas_call | solution.py:743

commit v8 on v7

--- a/solution.py
+++ b/solution.py
@@ -15,6 +15,7 @@
 ZS = 4
 PARTS = 4
 PCOLS = 2 * KVH * HD // PARTS
+ORDER = (2, 3, 0, 1)
 LOW = jnp.bfloat16
 FULL = jnp.float32
 MESH = pl.DeviceIdType.MESH
@@ -441,6 +442,26 @@
             at = slice(first + j * HD, first + (j + 1) * HD)
             wl_v[at, :] = (s_v[at, :] * inverse).astype(LOW)
 
+    def value_grad(h, b):
+        r0 = b * QBLK
+        first, keys = span(b)
+        acc[1, 0:keys, :] += jnp.dot(
+            wl_v[first : first + keys, :],
+            qd_r[h, 1, r0 : r0 + QBLK, :],
+            preferred_element_type=FULL,
+        )
+
+    def send_terms(part, first_block, last_block):
+        for j in range(first_block, last_block):
+            term = acc[part, j * rows : (j + 1) * rows, :]
+            if part == 0:
+                term = term * inv_root
+            dl_s[j, part] = term.astype(LOW)
+
+            @pl.when(me != j)
+            def _():
+                dl_copy(part, j).start()
+
     def attend(h, b):
         r0 = b * QBLK
         first, keys = span(b)
@@ -461,7 +482,6 @@
             at = slice(first + j * HD, first + (j + 1) * HD)
             ds_v[at, :] = (s_v[at, :] * inverse * (pg_v[at, :] - delta)).astype(LOW)
         all_keys = slice(first, first + keys)
-        acc[1, 0:keys, :] += jnp.dot(wl_v[all_keys, :], do_blk, preferred_element_type=FULL)
         acc[0, 0:keys, :] += jnp.dot(ds_v[all_keys, :], q_blk, preferred_element_type=FULL)
 
     def query_grad(b):
@@ -484,8 +504,12 @@
             weigh(h, b)
         settle(qd_r.at[h, 1], in_recv.at[h, 1])
 
+        for b in reversed(range(blocks)):
+            value_grad(h, b)
+
         @pl.when(h == heads - 1)
         def _():
+            send_terms(1, 0, group_size)
             send_dq(0)
 
         for b in reversed(range(blocks)):
@@ -493,17 +517,7 @@
 
             @pl.when(h == heads - 1)
             def _():
-                for part in range(2):
-                    for j in range(b * per_block, (b + 1) * per_block):
-                        at = slice(j * rows, (j + 1) * rows)
-                        term = acc[part, at, :]
-                        if part == 0:
-                            term = term * inv_root
-                        dl_s[j, part] = term.astype(LOW)
-
-                        @pl.when(me != j)
-                        def _():
-                            dl_copy(part, j).start()
+                send_terms(0, b * per_block, (b + 1) * per_block)
 
         for b in range(blocks):
             query_grad(b)
@@ -513,28 +527,35 @@
     each(0, heads, one_head)
 
     dl_r[me] = dl_s[me]
-    for b in range(group_size):
-        dg_s[b] = dl_s[sources[b]]
 
     def merge(received, part, g):
         return (
             received[g, part].astype(FULL) + received[KVH + g, part].astype(FULL)
         ).astype(LOW)
 
-    for part in range(PARTS):
+    last = ORDER[-1]
+
+    def gather(part):
         which = part * PCOLS // kvw
-        if part * PCOLS % kvw == 0:
-            settle(dl_r.at[seven, which], dl_recv.at[which])
         for i in range(PCOLS // HD):
             dkv_all[y * 2 + core, part, :, i * HD : (i + 1) * HD] = merge(
                 dl_r, which, (part * PCOLS % kvw) // HD + i
             )
-        for k in range(3 if part == PARTS - 1 else 2):
+        for k in range(3 if part == last else 2):
             ya_copy(part, k, True).start()
         yc_copy(part, 0, True).start()
 
+    settle(dl_r.at[seven, 1], dl_recv.at[1])
+    for part in ORDER[: PARTS // 2]:
+        gather(part)
+    send_dq(1)
+    for b in range(group_size):
+        dg_s[b] = dl_s[sources[b]]
+    settle(dl_r.at[seven, 0], dl_recv.at[0])
+    for part in ORDER[PARTS // 2 :]:
+        gather(part)
+
     each(1, group_size, lambda o: dg_copy(o, True).start())
-    each(1, heads, send_dq)
     settle(kv_r.at[:, pl.ds(0, others), :], kv_send)
     settle(qd_r.at[:, :, pl.ds(0, others), :], in_send)
     settle(hid_s.at[pl.ds(0, column - 1)], hid_send)
@@ -543,12 +564,12 @@
     def pass_on(part):
         for k in range(2):
             ya_copy(part, k, False).wait_recv()
-            if part < PARTS - 1:
+            if part != last:
                 yf_copy(part, k, True).start()
             yc_copy(part, 1 if k else ys - 1, True).start()
 
     def hand_far(part):
-        if part < PARTS - 1:
+        if part != last:
             settle(dkv_all.at[0, part], yf_recv.at[part])
         else:
             ya_copy(part, 2, False).wait_recv()
@@ -567,12 +588,14 @@
                 prod_s[part] = term.astype(LOW)
         each(1, summed_over, lambda o: rs_copy(part, o).start())
 
-    pass_on(0)
-    for part in range(PARTS):
-        if part + 1 < PARTS:
-            pass_on(part + 1)
+    pass_on(ORDER[0])
+    for i, part in enumerate(ORDER):
+        if i + 1 < PARTS:
+            pass_on(ORDER[i + 1])
         hand_far(part)
         multiply(part)
+        if i + 2 < heads:
+            send_dq(i + 2)
 
     dg_r[me] = dg_s[me]
     settle(dg_r.at[seven], dg_recv)
@@ -602,7 +625,7 @@
 
     norm = 1.0 / math.sqrt(total * replica_count)
     own = pl.ds(pl.multiple_of((me * 2 + x_hi) * piece, piece), piece)
-    for part in range(PARTS):
+    for part in ORDER:
         settle(rs_r.at[part, pl.ds(0, summed_over - 1)], rs_recv.at[part])
         summed = prod[part, own, :]
         for o in range(1, summed_over):
@@ -700,7 +723,7 @@
         dma,
         dma((PARTS, 3)),
         dma,
-        dma((PARTS - 1,)),
+        dma((PARTS,)),
         dma,
         dma((PARTS, ys)),
         dma,

time: 83 us -> 87.2 us (1.051)
  Pallas kernels: 82.1 us -> 86.4 us
    pallas_call x1, Pallas kernels: 79.5 us -> 83.8 us  [on_device(): pl.pallas_call(kernel, out_shape=out_shape, in_specs=[smem, smem, smem] +...]
where the time goes in v8:
time: 87.2 us; the launch traced here: 87 us
  Pallas kernels  86.4 us (99%)
    pallas_call x1, Pallas kernels, on_device(): pl.pallas_call(kernel, out_shape=out_shape, in_specs=[smem, smem, smem] +...  83.8 us
    pallas_call x1, Pallas kernels, on_device(): pl.pallas_call(hand_over, out_shape=out_shape, in_specs=[anywhere] * 4, o...  2.55 us

profile of v8, /device:TPU:1, one launch (start us, length us, event | category | flops | bytes accessed | tf_op | source)
XLA Modules:
  0.0 87.0 jit_solution(9246353555737834437)
XLA Ops:
  0.6 83.8 %layer.1 = (bf16[128,4096]{1,0:T(8,128)(2,1)}, bf16[128,4096]{1,0:T(8,128)(2,1)}, bf16[32,512]{1,0:T(8,128)(2,1)}, bf16[32,512]{1,0:T(8,128)(2,1)}) custom-call(s32[1,8]{1,0:T(1,128)} %refs_0_.1, s32[1,8]{1,0:T(1,128)} %refs_1_.1, s32[1,8]{1,0:T(1,128)} %refs_2_.1, bf16[128,4096]{1,0:T(8,128)(2,1)} %bitcast.5, bf16[128,4096]{1,0:T(8,128)(2,1)} %bitcast.6, ...), custom_call_target="tpu_custom_call" | custom-call | tf_op jit(solution)/shard_map/layer/pallas_call | solution.py:746
  84.5 2.5 %hand_over.1 = (bf16[128,4096]{1,0:T(8,128)(2,1)}, bf16[128,4096]{1,0:T(8,128)(2,1)}, bf16[32,512]{1,0:T(8,128)(2,1)}, bf16[32,512]{1,0:T(8,128)(2,1)}) custom-call(bf16[128,4096]{1,0:T(8,128)(2,1)} %get-tuple-element.12.refs_0_, bf16[128,4096]{1,0:T(8,128)(2,1)} %get-tuple-element.13.refs_1_, bf16[32,512]{1,0:T(8,128)(2,1)} %get-tuple-element.14.refs_2_, ...), custom_call_target="tpu_custom_call" | custom-call | tf_op jit(solution)/shard_map/hand_over/pallas_call | solution.py:766

commit v9 on v8

--- a/solution.py
+++ b/solution.py
@@ -548,7 +548,6 @@
     settle(dl_r.at[seven, 1], dl_recv.at[1])
     for part in ORDER[: PARTS // 2]:
         gather(part)
-    send_dq(1)
     for b in range(group_size):
         dg_s[b] = dl_s[sources[b]]
     settle(dl_r.at[seven, 0], dl_recv.at[0])
@@ -556,6 +555,7 @@
         gather(part)
 
     each(1, group_size, lambda o: dg_copy(o, True).start())
+    each(1, heads, send_dq)
     settle(kv_r.at[:, pl.ds(0, others), :], kv_send)
     settle(qd_r.at[:, :, pl.ds(0, others), :], in_send)
     settle(hid_s.at[pl.ds(0, column - 1)], hid_send)
@@ -594,8 +594,6 @@
             pass_on(ORDER[i + 1])
         hand_far(part)
         multiply(part)
-        if i + 2 < heads:
-            send_dq(i + 2)
 
     dg_r[me] = dg_s[me]
     settle(dg_r.at[seven], dg_recv)

time: 87.2 us -> 82.2 us (0.943); the launches traced: 87 us -> 80.8 us
  Pallas kernels: 86.4 us -> 80.2 us
    pallas_call x1, Pallas kernels: 83.8 us -> 77.6 us  [on_device(): pl.pallas_call(kernel, out_shape=out_shape, in_specs=[smem, smem, smem] +...]
where the time goes in v9:
time: 82.2 us; the launch traced here: 80.8 us
  Pallas kernels  80.2 us (98%)
    pallas_call x1, Pallas kernels, on_device(): pl.pallas_call(kernel, out_shape=out_shape, in_specs=[smem, smem, smem] +...  77.6 us
    pallas_call x1, Pallas kernels, on_device(): pl.pallas_call(hand_over, out_shape=out_shape, in_specs=[anywhere] * 4, o...  2.55 us

profile of v9, /device:TPU:1, one launch (start us, length us, event | category | flops | bytes accessed | tf_op | source)
XLA Modules:
  0.0 80.8 jit_solution(15556609569566678575)
XLA Ops:
  0.6 77.6 %layer.1 = (bf16[128,4096]{1,0:T(8,128)(2,1)}, bf16[128,4096]{1,0:T(8,128)(2,1)}, bf16[32,512]{1,0:T(8,128)(2,1)}, bf16[32,512]{1,0:T(8,128)(2,1)}) custom-call(s32[1,8]{1,0:T(1,128)} %refs_0_.1, s32[1,8]{1,0:T(1,128)} %refs_1_.1, s32[1,8]{1,0:T(1,128)} %refs_2_.1, bf16[128,4096]{1,0:T(8,128)(2,1)} %bitcast.5, bf16[128,4096]{1,0:T(8,128)(2,1)} %bitcast.6, ...), custom_call_target="tpu_custom_call" | custom-call | tf_op jit(solution)/shard_map/layer/pallas_call | solution.py:744
  78.3 2.5 %hand_over.1 = (bf16[128,4096]{1,0:T(8,128)(2,1)}, bf16[128,4096]{1,0:T(8,128)(2,1)}, bf16[32,512]{1,0:T(8,128)(2,1)}, bf16[32,512]{1,0:T(8,128)(2,1)}) custom-call(bf16[128,4096]{1,0:T(8,128)(2,1)} %get-tuple-element.12.refs_0_, bf16[128,4096]{1,0:T(8,128)(2,1)} %get-tuple-element.13.refs_1_, bf16[32,512]{1,0:T(8,128)(2,1)} %get-tuple-element.14.refs_2_, ...), custom_call_target="tpu_custom_call" | custom-call | tf_op jit(solution)/shard_map/hand_over/pallas_call | solution.py:764

commit v10 on v9

--- a/solution.py
+++ b/solution.py
@@ -15,6 +15,7 @@
 ZS = 4
 PARTS = 4
 PCOLS = 2 * KVH * HD // PARTS
+TWO_STEP = (2,)
 ORDER = (2, 3, 0, 1)
 LOW = jnp.bfloat16
 FULL = jnp.float32
@@ -68,6 +69,7 @@
     dkv_all,
     prod,
     prod_s,
+    rx_r,
     rs_r,
     gh_v,
     begin_v,
@@ -92,6 +94,8 @@
     yf_recv,
     yc_send,
     yc_recv,
+    rx_send,
+    rx_recv,
     rs_send,
     rs_recv,
     gh_sem,
@@ -110,6 +114,7 @@
     wide = heads * HD
     kvw = KVH * HD
     piece = width // (group_size * replica_count)
+    half_rows = group_size * piece
     inv_root = 1.0 / math.sqrt(HD)
     exp_scale = inv_root / math.log(2.0)
     blocks = total // QBLK
@@ -169,6 +174,8 @@
         ),
     )
 
+    across = {"grp": lax.rem(me + ZS, group_size), "dp": place(y, 1 - x_hi, core)}
+
     def q_copy(h, o, to):
         dest = peer(o)
         at = rows_of(me if to else origin(o))
@@ -296,7 +303,7 @@
 
     def rs_copy(part, o):
         dest = sum_peer(o)
-        at = dest["grp"] * 2 + lax.rem(x_hi + o // group_size, 2)
+        at = lax.rem(x_hi + o // group_size, 2) * group_size + dest["grp"]
         return pltpu.make_async_remote_copy(
             src_ref=prod_s.at[part, pl.ds(pl.multiple_of(at * piece, piece), piece), :],
             dst_ref=rs_r.at[part, o],
@@ -311,6 +318,16 @@
 
     others = total - rows
     seven = pl.ds(0, group_size - 1)
+
+    def rx_copy(part):
+        return pltpu.make_async_remote_copy(
+            src_ref=prod_s.at[part, pl.ds((1 - x_hi) * half_rows, half_rows), :],
+            dst_ref=rx_r.at[part],
+            send_sem=rx_send,
+            recv_sem=rx_recv.at[part],
+            device_id=across,
+            device_id_type=MESH,
+        )
 
     def own_q(h):
         return pltpu.make_async_copy(
@@ -363,7 +380,7 @@
         g = t // ys
         to_y = lax.rem(t, ys)
         for xh in range(2):
-            at = pl.ds(pl.multiple_of((g * 2 + xh) * piece, piece), piece)
+            at = pl.ds(pl.multiple_of((xh * group_size + g) * piece, piece), piece)
             for c in range(2):
                 hid_s[to_y * 2 + c, at, :] = turned[(xh * 2 + c) * piece :][:piece]
 
@@ -510,7 +527,6 @@
         @pl.when(h == heads - 1)
         def _():
             send_terms(1, 0, group_size)
-            send_dq(0)
 
         for b in reversed(range(blocks)):
             attend(h, b)
@@ -526,6 +542,7 @@
 
     each(0, heads, one_head)
 
+    send_dq(0)
     dl_r[me] = dl_s[me]
 
     def merge(received, part, g):
@@ -586,7 +603,18 @@
             prod[part] = term
             if k == 2:
                 prod_s[part] = term.astype(LOW)
-        each(1, summed_over, lambda o: rs_copy(part, o).start())
+        if part in TWO_STEP:
+            rx_copy(part).start()
+        else:
+            each(1, summed_over, lambda o: rs_copy(part, o).start())
+
+    def combine(part):
+        settle(rx_r.at[part], rx_recv.at[part])
+        at = pl.ds(x_hi * half_rows, half_rows)
+        both = prod[part, at, :] + rx_r[part].astype(FULL)
+        prod[part, at, :] = both
+        prod_s[part, at, :] = both.astype(LOW)
+        each(1, group_size, lambda o: rs_copy(part, o).start())
 
     pass_on(ORDER[0])
     for i, part in enumerate(ORDER):
@@ -594,6 +622,8 @@
             pass_on(ORDER[i + 1])
         hand_far(part)
         multiply(part)
+        if i > 0 and ORDER[i - 1] in TWO_STEP:
+            combine(ORDER[i - 1])
 
     dg_r[me] = dg_s[me]
     settle(dg_r.at[seven], dg_recv)
@@ -622,18 +652,23 @@
     settle(dkv_all.at[pl.ds(0, ys)], yc_send)
 
     norm = 1.0 / math.sqrt(total * replica_count)
-    own = pl.ds(pl.multiple_of((me * 2 + x_hi) * piece, piece), piece)
+    own = pl.ds(pl.multiple_of((x_hi * group_size + me) * piece, piece), piece)
     for part in ORDER:
-        settle(rs_r.at[part, pl.ds(0, summed_over - 1)], rs_recv.at[part])
+        senders = group_size if part in TWO_STEP else summed_over
+        settle(rs_r.at[part, pl.ds(0, senders - 1)], rs_recv.at[part])
         summed = prod[part, own, :]
-        for o in range(1, summed_over):
+        for o in range(1, senders):
             summed = summed + rs_r[part, o].astype(FULL)
         result = grad_value if part * PCOLS >= kvw else grad_key
         at = part * PCOLS % kvw
         result[:, at : at + PCOLS] = (summed * norm).astype(LOW)
 
     gh_out.wait()
-    settle(rs_r.at[:, pl.ds(0, summed_over - 1)], rs_send)
+    for part in range(PARTS):
+        senders = group_size if part in TWO_STEP else summed_over
+        settle(rs_r.at[part, pl.ds(0, senders - 1)], rs_send)
+    for part in TWO_STEP:
+        settle(rx_r.at[part], rx_send)
 
 
 def hand_over(*refs):
@@ -700,6 +735,7 @@
         pltpu.VMEM((column, PARTS, rows, PCOLS), LOW),
         pltpu.VMEM((PARTS, chunk, PCOLS), FULL),
         pltpu.VMEM((PARTS, chunk, PCOLS), LOW),
+        pltpu.VMEM((PARTS, chunk // 2, PCOLS), LOW),
         pltpu.VMEM((PARTS, 2 * group_size, piece, PCOLS), LOW),
         pltpu.VMEM((rows, width), LOW),
         pltpu.VMEM((1, total), jnp.int32),
@@ -724,6 +760,8 @@
         dma((PARTS,)),
         dma,
         dma((PARTS, ys)),
+        dma,
+        dma((PARTS,)),
         dma,
         dma((PARTS,)),
         dma,

time: 82.2 us -> 80.3 us (0.977); the launches traced: 80.8 us -> 80.1 us
  no operation moved by 1% of the time
where the time goes in v10:
time: 80.3 us; the launch traced here: 80.1 us
  Pallas kernels  79.4 us (99%)
    pallas_call x1, Pallas kernels, on_device(): pl.pallas_call(kernel, out_shape=out_shape, in_specs=[smem, smem, smem] +...  76.9 us
    pallas_call x1, Pallas kernels, on_device(): pl.pallas_call(hand_over, out_shape=out_shape, in_specs=[anywhere] * 4, o...  2.55 us

profile of v10, /device:TPU:1, one launch (start us, length us, event | category | flops | bytes accessed | tf_op | source)
XLA Modules:
  0.0 80.1 jit_solution(1861295276475912180)
XLA Ops:
  0.6 76.9 %layer.1 = (bf16[128,4096]{1,0:T(8,128)(2,1)}, bf16[128,4096]{1,0:T(8,128)(2,1)}, bf16[32,512]{1,0:T(8,128)(2,1)}, bf16[32,512]{1,0:T(8,128)(2,1)}) custom-call(s32[1,8]{1,0:T(1,128)} %refs_0_.1, s32[1,8]{1,0:T(1,128)} %refs_1_.1, s32[1,8]{1,0:T(1,128)} %refs_2_.1, bf16[128,4096]{1,0:T(8,128)(2,1)} %bitcast.5, bf16[128,4096]{1,0:T(8,128)(2,1)} %bitcast.6, ...), custom_call_target="tpu_custom_call" | custom-call | tf_op jit(solution)/shard_map/layer/pallas_call | solution.py:782
  77.5 2.5 %hand_over.1 = (bf16[128,4096]{1,0:T(8,128)(2,1)}, bf16[128,4096]{1,0:T(8,128)(2,1)}, bf16[32,512]{1,0:T(8,128)(2,1)}, bf16[32,512]{1,0:T(8,128)(2,1)}) custom-call(bf16[128,4096]{1,0:T(8,128)(2,1)} %get-tuple-element.12.refs_0_, bf16[128,4096]{1,0:T(8,128)(2,1)} %get-tuple-element.13.refs_1_, bf16[32,512]{1,0:T(8,128)(2,1)} %get-tuple-element.14.refs_2_, ...), custom_call_target="tpu_custom_call" | custom-call | tf_op jit(solution)/shard_map/hand_over/pallas_call | solution.py:802

commit v11 on v10

--- a/solution.py
+++ b/solution.py
@@ -542,7 +542,10 @@
 
     each(0, heads, one_head)
 
-    send_dq(0)
+    each(0, 2, send_dq)
+    for b in range(group_size):
+        dg_s[b] = dl_s[sources[b]]
+    each(1, group_size, lambda o: dg_copy(o, True).start())
     dl_r[me] = dl_s[me]
 
     def merge(received, part, g):
@@ -565,14 +568,11 @@
     settle(dl_r.at[seven, 1], dl_recv.at[1])
     for part in ORDER[: PARTS // 2]:
         gather(part)
-    for b in range(group_size):
-        dg_s[b] = dl_s[sources[b]]
     settle(dl_r.at[seven, 0], dl_recv.at[0])
     for part in ORDER[PARTS // 2 :]:
         gather(part)
 
-    each(1, group_size, lambda o: dg_copy(o, True).start())
-    each(1, heads, send_dq)
+    each(2, heads, send_dq)
     settle(kv_r.at[:, pl.ds(0, others), :], kv_send)
     settle(qd_r.at[:, :, pl.ds(0, others), :], in_send)
     settle(hid_s.at[pl.ds(0, column - 1)], hid_send)

time: 80.3 us -> 80 us (level)
  no operation moved by 1% of the time
where the time goes in v11:
time: 80 us; the launch traced here: 79.5 us
  Pallas kernels  78.8 us (98%)
    pallas_call x1, Pallas kernels, on_device(): pl.pallas_call(kernel, out_shape=out_shape, in_specs=[smem, smem, smem] +...  76.3 us
    pallas_call x1, Pallas kernels, on_device(): pl.pallas_call(hand_over, out_shape=out_shape, in_specs=[anywhere] * 4, o...  2.55 us

profile of v11, /device:TPU:1, one launch (start us, length us, event | category | flops | bytes accessed | tf_op | source)
XLA Modules:
  0.0 79.5 jit_solution(299051532004561819)
XLA Ops:
  0.6 76.3 %layer.1 = (bf16[128,4096]{1,0:T(8,128)(2,1)}, bf16[128,4096]{1,0:T(8,128)(2,1)}, bf16[32,512]{1,0:T(8,128)(2,1)}, bf16[32,512]{1,0:T(8,128)(2,1)}) custom-call(s32[1,8]{1,0:T(1,128)} %refs_0_.1, s32[1,8]{1,0:T(1,128)} %refs_1_.1, s32[1,8]{1,0:T(1,128)} %refs_2_.1, bf16[128,4096]{1,0:T(8,128)(2,1)} %bitcast.5, bf16[128,4096]{1,0:T(8,128)(2,1)} %bitcast.6, ...), custom_call_target="tpu_custom_call" | custom-call | tf_op jit(solution)/shard_map/layer/pallas_call | solution.py:782
  76.9 2.5 %hand_over.1 = (bf16[128,4096]{1,0:T(8,128)(2,1)}, bf16[128,4096]{1,0:T(8,128)(2,1)}, bf16[32,512]{1,0:T(8,128)(2,1)}, bf16[32,512]{1,0:T(8,128)(2,1)}) custom-call(bf16[128,4096]{1,0:T(8,128)(2,1)} %get-tuple-element.12.refs_0_, bf16[128,4096]{1,0:T(8,128)(2,1)} %get-tuple-element.13.refs_1_, bf16[32,512]{1,0:T(8,128)(2,1)} %get-tuple-element.14.refs_2_, ...), custom_call_target="tpu_custom_call" | custom-call | tf_op jit(solution)/shard_map/hand_over/pallas_call | solution.py:802

commit v12 on v11

--- a/solution.py
+++ b/solution.py
@@ -542,7 +542,7 @@
 
     each(0, heads, one_head)
 
-    each(0, 2, send_dq)
+    each(0, heads, send_dq)
     for b in range(group_size):
         dg_s[b] = dl_s[sources[b]]
     each(1, group_size, lambda o: dg_copy(o, True).start())
@@ -572,7 +572,6 @@
     for part in ORDER[PARTS // 2 :]:
         gather(part)
 
-    each(2, heads, send_dq)
     settle(kv_r.at[:, pl.ds(0, others), :], kv_send)
     settle(qd_r.at[:, :, pl.ds(0, others), :], in_send)
     settle(hid_s.at[pl.ds(0, column - 1)], hid_send)

time: 80 us -> 80.1 us (level)
  no operation moved by 1% of the time
where the time goes in v12:
time: 80.1 us; the launch traced here: 79.5 us
  Pallas kernels  78.9 us (99%)
    pallas_call x1, Pallas kernels, on_device(): pl.pallas_call(kernel, out_shape=out_shape, in_specs=[smem, smem, smem] +...  76.3 us
    pallas_call x1, Pallas kernels, on_device(): pl.pallas_call(hand_over, out_shape=out_shape, in_specs=[anywhere] * 4, o...  2.55 us

profile of v12, /device:TPU:1, one launch (start us, length us, event | category | flops | bytes accessed | tf_op | source)
XLA Modules:
  0.0 79.5 jit_solution(11276693400056441410)
XLA Ops:
  0.6 76.3 %layer.1 = (bf16[128,4096]{1,0:T(8,128)(2,1)}, bf16[128,4096]{1,0:T(8,128)(2,1)}, bf16[32,512]{1,0:T(8,128)(2,1)}, bf16[32,512]{1,0:T(8,128)(2,1)}) custom-call(s32[1,8]{1,0:T(1,128)} %refs_0_.1, s32[1,8]{1,0:T(1,128)} %refs_1_.1, s32[1,8]{1,0:T(1,128)} %refs_2_.1, bf16[128,4096]{1,0:T(8,128)(2,1)} %bitcast.5, bf16[128,4096]{1,0:T(8,128)(2,1)} %bitcast.6, ...), custom_call_target="tpu_custom_call" | custom-call | tf_op jit(solution)/shard_map/layer/pallas_call | solution.py:781
  77.0 2.5 %hand_over.1 = (bf16[128,4096]{1,0:T(8,128)(2,1)}, bf16[128,4096]{1,0:T(8,128)(2,1)}, bf16[32,512]{1,0:T(8,128)(2,1)}, bf16[32,512]{1,0:T(8,128)(2,1)}) custom-call(bf16[128,4096]{1,0:T(8,128)(2,1)} %get-tuple-element.12.refs_0_, bf16[128,4096]{1,0:T(8,128)(2,1)} %get-tuple-element.13.refs_1_, bf16[32,512]{1,0:T(8,128)(2,1)} %get-tuple-element.14.refs_2_, ...), custom_call_target="tpu_custom_call" | custom-call | tf_op jit(solution)/shard_map/hand_over/pallas_call | solution.py:801
